TPU v7x, 32 devices: a whole 2x2x4 slice. The times are simulated.
32 devices in a mesh: dp: 8 (over z, y), cam: 4 (over x, core).
Axes of the slice: x: 2, y: 2, z: 4, core: 2. Of those that a mesh axis runs over, the one named last changes fastest.
Arguments:
- tokens: bfloat16 [32, 4, 304, 512], P('dp', 'cam'), may hold values from -6 to 6
- out_grad: bfloat16 [32, 4, 304, 512], P('dp', 'cam'), may hold values from -6 to 6
- joint_state: float32 [32, 1, 14], P('dp'), may hold values from -4 to 4
- joint_mask: int32 [32, 1, 14], P('dp'), may hold values from 0 to 1, as said below
- attn_master: float32 [4, 512, 512], P(None, ('dp', 'cam')), may hold values from -0.25 to 0.25
- attn_first: float32 [4, 512, 512], P(None, ('dp', 'cam'))
- attn_second: float32 [4, 512, 512], P(None, ('dp', 'cam'))
- attn_average: float32 [4, 512, 512], P(None, ('dp', 'cam')), may hold values from -0.25 to 0.25
- ffn_master: float32 [2, 512, 3200], P(None, ('dp', 'cam')), may hold values from -0.25 to 0.25
- ffn_first: float32 [2, 512, 3200], P(None, ('dp', 'cam'))
- ffn_second: float32 [2, 512, 3200], P(None, ('dp', 'cam'))
- ffn_average: float32 [2, 512, 3200], P(None, ('dp', 'cam')), may hold values from -0.25 to 0.25
- small_params: float32 [14464], replicated
- small_first: float32 [14464], replicated
- small_second: float32 [14464], replicated
- small_average: float32 [14464], replicated, may hold values from -3 to 3
Outputs:
- block_output: bfloat16 [32, 4, 304, 512], P('dp', 'cam')
- input_grad: float32 [32, 4, 304, 512], P('dp', 'cam')
- new_attn: float32 [4, 512, 512], P(None, ('dp', 'cam'))
- new_attn_first: float32 [4, 512, 512], P(None, ('dp', 'cam'))
- new_attn_second: float32 [4, 512, 512], P(None, ('dp', 'cam'))
- new_attn_average: float32 [4, 512, 512], P(None, ('dp', 'cam'))
- new_ffn: float32 [2, 512, 3200], P(None, ('dp', 'cam'))
- new_ffn_first: float32 [2, 512, 3200], P(None, ('dp', 'cam'))
- new_ffn_second: float32 [2, 512, 3200], P(None, ('dp', 'cam'))
- new_ffn_average: float32 [2, 512, 3200], P(None, ('dp', 'cam'))
- new_small: float32 [14464], replicated
- new_small_first: float32 [14464], replicated
- new_small_second: float32 [14464], replicated
- new_small_average: float32 [14464], replicated
Inputs may be any that keep to these rules, and one draw needn't show every extreme that they name: `joint_mask`: each item's mask is one on its first 7 joints and zero on the rest, or one on all 14 joints.
All inputs are finite; a program needn't handle non-finite values.
Results may differ from a plain program's by a relative error of at most 0.015.
The roundings to bfloat16 on the way count: a program that leaves them out, or rounds other values in their place, can miss the bound.
Values may be sent and summed in bfloat16 or wider, within the bound.
No kernel may reach another device: no remote copies, remote signals or barrier semaphores. Data moves between devices by JAX's collectives and lax.ppermute only.
A program may use at most 192 MiB of HBM per device.

v0:
```python
import jax
import jax.numpy as jnp
from jax import lax
from jax.sharding import PartitionSpec as P

D = 512
HEADS = 8
NJ = 14
ADAM_STEP = 10
HD = 64


highest = lax.Precision.HIGHEST
norm_eps = 1e-05
beta_first = 0.5
beta_second = 0.5
adam_eps = 1e-08
rate_matrix = 0.02
rate_small = 0.05
decay_matrix = 0.1
ema_decay = 0.75


def partner(value, axis, apart):
    mask = 2**apart
    pairs = [(source, source ^ mask) for source in range(lax.axis_size(axis))]
    return lax.ppermute(value, axis, pairs)


def norm_rows(values, gain_row, shift_row):
    centred = values - jnp.mean(values, axis=-1, keepdims=True)
    spread = jnp.mean(centred * centred, axis=-1, keepdims=True)
    return centred * lax.rsqrt(spread + norm_eps) * gain_row + shift_row


def smooth_gate(values):
    return jax.nn.gelu(values, approximate=False)


def adam_update(master, grad_total, first_old, second_old, average_old, rate, decay):
    first_new = beta_first * first_old + (1.0 - beta_first) * grad_total
    second_new = beta_second * second_old + (1.0 - beta_second) * grad_total * grad_total
    first_hat = first_new / (1.0 - beta_first**ADAM_STEP)
    second_hat = second_new / (1.0 - beta_second**ADAM_STEP)
    master_new = master - rate * (first_hat / (jnp.sqrt(second_hat) + adam_eps) + decay * master)
    average_new = ema_decay * average_old + (1.0 - ema_decay) * master_new
    return (master_new, first_new, second_new, average_new)


def contract_last(left_side, right_side):
    return lax.dot_general(
        left_side, right_side, (((1,), (1,)), ((), ())), preferred_element_type=jnp.float32
    )


def head_scores(query_head, key_head):
    score_scale = query_head.shape[-1] ** (-0.5)
    return (
        jnp.einsum("iqd,ikd->iqk", query_head, key_head, preferred_element_type=jnp.float32)
        * score_scale
    )


def attend_head(operands):
    query_head, key_head, value_head = operands
    scores = head_scores(query_head, key_head)
    highest_score = jnp.max(scores, axis=-1, keepdims=True)
    log_total = highest_score + jnp.log(
        jnp.sum(jnp.exp(scores - highest_score), axis=-1, keepdims=True)
    )
    probs_low = jnp.exp(scores - log_total).astype(jnp.bfloat16)
    mixed_head = jnp.einsum(
        "iqk,ikd->iqd", probs_low, value_head, preferred_element_type=jnp.float32
    ).astype(jnp.bfloat16)
    return (mixed_head, log_total)


def attend_back(operands):
    query_head, key_head, value_head, mixed_grad_head, log_total = operands
    score_scale = query_head.shape[-1] ** (-0.5)
    probs = jnp.exp(head_scores(query_head, key_head) - log_total)
    probs_low = probs.astype(jnp.bfloat16)
    prob_grad = jnp.einsum(
        "iqd,ikd->iqk", mixed_grad_head, value_head, preferred_element_type=jnp.float32
    )
    score_grad = (probs * (prob_grad - jnp.sum(probs * prob_grad, axis=-1, keepdims=True))).astype(
        jnp.bfloat16
    )
    query_grad_head = (
        jnp.einsum("iqk,ikd->iqd", score_grad, key_head, preferred_element_type=jnp.float32)
        * score_scale
    ).astype(jnp.bfloat16)
    key_grad_head = (
        jnp.einsum("iqk,iqd->ikd", score_grad, query_head, preferred_element_type=jnp.float32)
        * score_scale
    )
    value_grad_head = jnp.einsum(
        "iqk,iqd->ikd", probs_low, mixed_grad_head, preferred_element_type=jnp.float32
    )
    return (query_grad_head, key_grad_head, value_grad_head)


def group_trade(pieces, cam_index, mover):
    for bit_index in range(2):
        axis_pos = 1 - bit_index
        upper_half = cam_index >> bit_index & 1 == 1
        first_half = lax.index_in_dim(pieces, 0, axis_pos, keepdims=False)
        second_half = lax.index_in_dim(pieces, 1, axis_pos, keepdims=False)
        keep_part = jnp.where(upper_half, second_half, first_half)
        send_part = jnp.where(upper_half, first_half, second_half)
        arrived = mover(send_part, bit_index)
        pieces = jnp.stack(
            [jnp.where(upper_half, arrived, keep_part), jnp.where(upper_half, keep_part, arrived)],
            axis=axis_pos,
        )
    return pieces


def local(
    tokens,
    out_grad,
    joint_state,
    joint_mask,
    attn_master,
    attn_first,
    attn_second,
    attn_average,
    ffn_master,
    ffn_first,
    ffn_second,
    ffn_average,
    small_params,
    small_first,
    small_second,
    small_average,
):
    cam_index = lax.axis_index("cam")
    camera_slot = cam_index % 4
    group_index = cam_index // 4
    items_here = tokens.shape[0]
    seg_len = tokens.shape[2]
    quarter = items_here // 4
    out_scale = (4 * seg_len / 3.0) ** 0.5
    attn_low = attn_master.astype(jnp.bfloat16)
    ffn_low = ffn_master.astype(jnp.bfloat16)
    attn_full, ffn_full = (
        lax.all_gather(attn_low, ("dp", "cam"), axis=1, tiled=True),
        lax.all_gather(ffn_low, ("dp", "cam"), axis=1, tiled=True),
    )
    vectors = small_params[: 8 * D].reshape(8, D)
    joint_rows = small_params[8 * D : (8 + NJ) * D].reshape(NJ, D)
    hidden_bias = small_params[(8 + NJ) * D :]
    state_rows = lax.dynamic_slice_in_dim(joint_state, group_index, 1, 1)[:, 0]
    mask_rows = lax.dynamic_slice_in_dim(joint_mask, group_index, 1, 1)[:, 0].astype(jnp.float32)
    active_rows = state_rows * mask_rows
    query_len = 4 * seg_len
    both_in = jnp.stack([tokens[:, 0], out_grad[:, 0]]).reshape(2, 2, 2, quarter, seg_len, D)
    both_in = jnp.moveaxis(both_in, 0, 2)

    def move_inputs(piece, bit_index):
        return partner(piece, "cam", bit_index)

    traded = group_trade(both_in, cam_index, move_inputs)
    whole_items = jnp.moveaxis(traded.reshape(4, 2, quarter, seg_len, D), 0, 2).reshape(
        2, quarter, query_len, D
    )
    seq_in = whole_items[0].astype(jnp.float32)
    cot_in = whole_items[1]
    joint_active = lax.dynamic_slice_in_dim(active_rows, camera_slot * quarter, quarter, 0)
    joint_on = jnp.float32(1.0)
    row_count = quarter * query_len
    joint_token = jnp.dot(joint_active, joint_rows, precision=highest) * joint_on
    summed_in = seq_in.at[:, 1].add(joint_token).reshape(row_count, D)
    rounded = summed_in.astype(jnp.bfloat16)
    projected = jnp.einsum(
        "td,jde->jte", rounded, attn_full[:3], preferred_element_type=jnp.float32
    )
    query_low = (projected[0] + vectors[0]).astype(jnp.bfloat16)
    key_low = projected[1].astype(jnp.bfloat16)
    value_low = (projected[2] + vectors[1]).astype(jnp.bfloat16)
    gathered = jnp.stack([key_low, value_low]).reshape(2, quarter, query_len, HEADS, HD)
    query_heads = jnp.moveaxis(query_low.reshape(quarter, query_len, HEADS, HD), 2, 0)
    key_heads = jnp.moveaxis(gathered[0], 2, 0)
    value_heads = jnp.moveaxis(gathered[1], 2, 0)
    mixed_heads, log_totals = lax.map(attend_head, (query_heads, key_heads, value_heads))
    mixed_low = jnp.moveaxis(mixed_heads, 0, 2).reshape(row_count, D)
    branch = (
        jnp.dot(mixed_low, attn_full[3], preferred_element_type=jnp.float32) * out_scale
        + vectors[2]
    )
    normed, first_norm_back = jax.vjp(norm_rows, summed_in + branch, vectors[3], vectors[4])
    normed_low = normed.astype(jnp.bfloat16)
    inner = jnp.dot(normed_low, ffn_full[0], preferred_element_type=jnp.float32) + hidden_bias
    activated, gate_back = jax.vjp(smooth_gate, inner)
    activated_low = activated.astype(jnp.bfloat16)
    output_branch = contract_last(activated_low, ffn_full[1]) + vectors[5]
    result, second_norm_back = jax.vjp(norm_rows, normed + output_branch, vectors[6], vectors[7])
    result_low = result.astype(jnp.bfloat16)
    cotangent = cot_in.astype(jnp.float32).reshape(row_count, D)
    middle_grad, gain_two_grad, shift_two_grad = second_norm_back(cotangent)
    branch_two_low = middle_grad.astype(jnp.bfloat16)
    down_grad = jnp.einsum(
        "td,tf->df", branch_two_low, activated_low, preferred_element_type=jnp.float32
    )
    (inner_grad,) = gate_back(
        jnp.dot(branch_two_low, ffn_full[1], preferred_element_type=jnp.float32)
    )
    inner_low = inner_grad.astype(jnp.bfloat16)
    up_grad = jnp.einsum("td,tf->df", normed_low, inner_low, preferred_element_type=jnp.float32)
    normed_grad = middle_grad + contract_last(inner_low, ffn_full[0])
    summed_grad, gain_one_grad, shift_one_grad = first_norm_back(normed_grad)
    branch_one_low = summed_grad.astype(jnp.bfloat16)
    out_proj_grad = (
        jnp.einsum("td,te->de", mixed_low, branch_one_low, preferred_element_type=jnp.float32)
        * out_scale
    )
    mixed_grad = (
        (contract_last(branch_one_low, attn_full[3]) * out_scale)
        .astype(jnp.bfloat16)
        .reshape(quarter, query_len, HEADS, HD)
    )
    mixed_grad_heads = jnp.moveaxis(mixed_grad, 2, 0)
    query_grad_heads, key_grad_heads, value_grad_heads = lax.map(
        attend_back, (query_heads, key_heads, value_heads, mixed_grad_heads, log_totals)
    )
    query_grad = jnp.moveaxis(query_grad_heads, 0, 2).reshape(row_count, D)
    key_part = jnp.moveaxis(key_grad_heads, 0, 2)
    value_part = jnp.moveaxis(value_grad_heads, 0, 2)
    owned_grads = jnp.stack([key_part, value_part]).reshape(2, row_count, D).astype(jnp.bfloat16)
    proj_grads = jnp.stack([query_grad, owned_grads[0], owned_grads[1]])
    proj_weight_grad = jnp.einsum(
        "td,jte->jde", rounded, proj_grads, preferred_element_type=jnp.float32
    )
    input_flat = summed_grad + jnp.einsum(
        "jte,jde->td", proj_grads, attn_full[:3], preferred_element_type=jnp.float32
    )
    joint_grad = input_flat.reshape(quarter, query_len, D)[:, 1] * joint_on

    def move_outputs(piece, bit_index):
        return partner(piece, "cam", bit_index)

    def move_input_grads(piece, bit_index):
        return partner(piece.astype(jnp.bfloat16), "cam", bit_index).astype(piece.dtype)

    out_pieces = jnp.moveaxis(result_low.reshape(quarter, 4, seg_len, D), 1, 0).reshape(
        2, 2, quarter, seg_len, D
    )
    grad_pieces = jnp.moveaxis(input_flat.reshape(quarter, 4, seg_len, D), 1, 0).reshape(
        2, 2, quarter, seg_len, D
    )
    block_output = group_trade(out_pieces, cam_index, move_outputs).reshape(tokens.shape)
    input_grad = group_trade(grad_pieces, cam_index, move_input_grads).reshape(tokens.shape)
    small_grad = jnp.concatenate(
        [
            jnp.sum(query_grad.astype(jnp.float32), axis=0),
            jnp.sum(owned_grads[1].astype(jnp.float32), axis=0),
            jnp.sum(branch_one_low.astype(jnp.float32), axis=0),
            gain_one_grad,
            shift_one_grad,
            jnp.sum(branch_two_low.astype(jnp.float32), axis=0),
            gain_two_grad,
            shift_two_grad,
            jnp.dot(joint_active.T, joint_grad, precision=highest).reshape(-1),
            jnp.sum(inner_low.astype(jnp.float32), axis=0),
        ]
    )
    small_total = lax.psum(small_grad, ("dp", "cam"))
    attn_grad = jnp.concatenate([proj_weight_grad, out_proj_grad[None]], axis=0)
    ffn_grad = jnp.stack([up_grad, down_grad])
    attn_shard, ffn_shard = (
        lax.psum_scatter(attn_grad, ("dp", "cam"), scatter_dimension=1, tiled=True),
        lax.psum_scatter(ffn_grad, ("dp", "cam"), scatter_dimension=1, tiled=True),
    )
    new_attn, new_attn_first, new_attn_second, new_attn_average = adam_update(
        attn_master, attn_shard, attn_first, attn_second, attn_average, rate_matrix, decay_matrix
    )
    new_ffn, new_ffn_first, new_ffn_second, new_ffn_average = adam_update(
        ffn_master, ffn_shard, ffn_first, ffn_second, ffn_average, rate_matrix, decay_matrix
    )
    new_small, new_small_first, new_small_second, new_small_average = adam_update(
        small_params, small_total, small_first, small_second, small_average, rate_small, 0.0
    )
    return (
        block_output,
        input_grad,
        new_attn,
        new_attn_first,
        new_attn_second,
        new_attn_average,
        new_ffn,
        new_ffn_first,
        new_ffn_second,
        new_ffn_average,
        new_small,
        new_small_first,
        new_small_second,
        new_small_average,
    )


def solution(mesh):
    in_specs = (
        P("dp", "cam", None, None),
        P("dp", "cam", None, None),
        P("dp", None, None),
        P("dp", None, None),
        P(None, ("dp", "cam"), None),
        P(None, ("dp", "cam"), None),
        P(None, ("dp", "cam"), None),
        P(None, ("dp", "cam"), None),
        P(None, ("dp", "cam"), None),
        P(None, ("dp", "cam"), None),
        P(None, ("dp", "cam"), None),
        P(None, ("dp", "cam"), None),
        P(),
        P(),
        P(),
        P(),
    )
    out_specs = (
        P("dp", "cam", None, None),
        P("dp", "cam", None, None),
        P(None, ("dp", "cam"), None),
        P(None, ("dp", "cam"), None),
        P(None, ("dp", "cam"), None),
        P(None, ("dp", "cam"), None),
        P(None, ("dp", "cam"), None),
        P(None, ("dp", "cam"), None),
        P(None, ("dp", "cam"), None),
        P(None, ("dp", "cam"), None),
        P(),
        P(),
        P(),
        P(),
    )
    return jax.shard_map(local, mesh=mesh, in_specs=in_specs, out_specs=out_specs, check_vma=False)
```

profile of v0, /device:TPU:0, one launch (start us, length us, event | category | flops | bytes accessed | tf_op | source)
XLA Modules:
  0.0 685.9 jit_solution(14476211692514867575)
XLA Ops:
  12.4 2.9 collective-permute-done
  18.2 2.9 collective-permute-start.1
  22.6 28.4 %collective-permute-done.1 = bf16[2,2,1,304,512]{4,3,1,0,2:T(8,128)(2,1)S(1)} collective-permute-done((bf16[2,2,1,304,512]{4,3,1,0,2:T(8,128)(2,1)S(1)}, bf16[2,2,1,304,512]{4,3,1,0,2:T(8,128)(2,1)S(1)}, u32[]{:S(2)}, u32[]{:S(2)}) %collective-permute-start.1) | collective-permute-done | bytes 1245216 | tf_op jit(solution)/shard_map/ppermute | solution.py:27
  51.1 2.4 select_bitcast_fusion.1
  57.9 13.8 %all-gather.3.cloned.1.call-done = bf16[4,512,512]{2,1,0:T(8,128)(2,1)} async-done(((bf16[4,16,512]{2,1,0:T(8,128)(2,1)}), bf16[4,512,512]{2,1,0:T(8,128)(2,1)}) %all-gather.3.cloned.1.call-update) | async-done | bytes 2097168 | tf_op jit(solution)/shard_map/all_gather | solution.py:147
  71.7 3.5 convolution_bitcast_fusion.2
  76.4 2.4 fusion.59
  78.8 2.1 copy.173
  82.2 3.8 copy.176
  87.5 3.3 copy.177
  90.8 2.4 copy.175
  93.2 3.7 copy.178
  98.1 49.5 %while.27 = (s32[]{:T(128)}, bf16[8,1,1216,64]{2,3,1,0:T(8,128)(2,1)}, f32[8,1,1216,1]{2,3,1,0:T(1,128)}, bf16[8,1,1216,64]{3,2,1,0:T(8,128)(2,1)}, bf16[8,1,121...) while((s32[]{:T(128)}, bf16[8,1,1216,64]{2,3,1,0:T(8,128)(2,1)}, ...), condition=%wide.region_3.4_spmd, body=%wide.region_0.3_spmd.sunk | while | flops 387484480 | bytes 18887768 | solution.py:185
  98.1 1.9 fusion.140
  100.9 2.7 fusion.141
  107.1 2.7 fusion.141
  113.3 2.7 fusion.141
  119.5 2.8 fusion.141
  125.7 2.7 fusion.141
  131.9 2.7 fusion.141
  138.1 2.7 fusion.141
  144.3 2.7 fusion.141
  149.1 3.2 fusion.109
  153.5 42.4 %multiply_convert_fusion.1 = (bf16[1216,3200]{1,0:T(8,128)(2,1)S(1)}, f32[1216,3200]{1,0:T(8,128)}, f32[1216,3200]{1,0:T(8,128)}) fusion(f32[3200]{0:T(1024)S(1)} %slice-done, bf16[2,512,3200]{2,1,0:T(8,128)(2,1)} %all-gather.5.cloned.1.call-done, f32[1216,512]{1,0:T(8,128)S(1)} %get-tuple-element.284, f32[512]{0:T(512)S(1)} %get-tuple-element.277, ...), kind=kOutput, calls=%fused_computation.60 | convolution fusion | flops 4244520960 | bytes 44705792 | tf_op jit(solution)/shard_map/dot_general | solution.py:193
  195.9 4.9 fusion.110
  204.2 2.4 add_add_fusion.1
  208.6 3.6 convert_reduce_fusion.4
  212.2 18.8 %convert_reduce_fusion = (f32[3200]{0:T(1024)S(1)}, bf16[1216,3200]{1,0:T(8,128)(2,1)}) fusion(f32[1216,3200]{1,0:T(8,128)} %get-tuple-element.254, f32[1216,3200]{1,0:T(8,128)} %get-tuple-element.285, bf16[1216,512]{1,0:T(8,128)(2,1)} %get-tuple-element.240, bf16[2,512,3200]{2,1,0:T(8,128)(2,1)} %all-gather.5.cloned.1.call-done), kind=kOutput, calls=%fused_computation.58 | convolution fusion | flops 4046844928 | bytes 43446784 | tf_op jit(solution)/shard_map/dot_general | solution.py:206
  231.0 10.4 %convolution_bitcast_fusion.1 = f32[1,512,3200]{2,1,0:T(8,128)} fusion(bf16[1216,3200]{1,0:T(8,128)(2,1)} %get-tuple-element.290, f32[1216,512]{1,0:T(8,128)S(1)} %get-tuple-element.284, f32[512]{0:T(512)S(1)} %get-tuple-element.277, f32[512]{0:T(512)S(1)} %get-tuple-element.278, f32[1216]{0:T(1024)S(1)} %fusion.94, f32[1216]{0:T(1024)S(1)} %broadcast_multiply_fusion.2), kind=kOutput, calls=%fused_computation.76 | convolution fusion | flops 3987701760 | bytes 16840192 | tf_op jit(solution)/shard_map/td,tf->df/dot_general | solution.py:209
  241.4 7.2 %multiply_reduce_fusion.1 = (f32[512]{0:T(512)S(1)}, f32[1216]{0:T(1024)S(1)}, f32[512]{0:T(512)S(1)}, f32[1216,512]{1,0:T(8,128)S(1)}) fusion(f32[1216,512]{1,0:T(8,128)S(1)} %get-tuple-element.284, f32[1216]{0:T(1024)S(1)} %fusion.94, f32[1216]{0:T(1024)S(1)} %broadcast_multiply_fusion.2, f32[512]{0:T(512)S(1)} %get-tuple-element.278, ...), kind=kOutput, calls=%fused_computation.112 | convolution fusion | flops 3990812416 | bytes 18555904 | tf_op jit(solution)/shard_map/dot_general | solution.py:51
  256.3 98.6 %while.28 = (s32[]{:T(128)}, bf16[8,1,1216,64]{2,3,1,0:T(8,128)(2,1)S(1)}, bf16[8,1,1216,64]{2,3,1,0:T(8,128)(2,1)}, bf16[8,1,1216,64]{2,3,1,0:T(8,128)(2,1)}, b...) while((s32[]{:T(128)}, ...), condition=%wide.region_14.15_spmd, body=%wide.region_12.14_spmd.sunk | while | flops 958401344 | bytes 47559536 | solution.py:223
  259.1 2.6 multiply_reduce_fusion.7
  264.4 2.7 fusion.152
  271.4 2.6 multiply_reduce_fusion.7
  276.7 2.6 fusion.152
  283.7 2.6 multiply_reduce_fusion.7
  289.0 2.7 fusion.152
  296.1 2.6 multiply_reduce_fusion.7
  301.3 2.7 fusion.152
  308.4 2.6 multiply_reduce_fusion.7
  313.6 2.7 fusion.152
  320.7 2.6 multiply_reduce_fusion.7
  325.9 2.7 fusion.152
  333.0 2.6 multiply_reduce_fusion.7
  338.2 2.6 fusion.152
  345.2 2.6 multiply_reduce_fusion.7
  350.5 2.7 fusion.152
  354.9 2.9 copy.189
  357.8 2.6 copy.188
  360.4 2.5 copy.187
  362.9 4.4 convolution_bitcast_fusion.4
  367.3 2.4 pad_maximum_fusion.1
  369.7 5.5 copy.199
  376.5 10.2 %convolution_bitcast_fusion = f32[1,512,3200]{2,1,0:T(8,128)} fusion(bf16[1216,512]{1,0:T(8,128)(2,1)S(1)} %copy-done.23, bf16[1216,3200]{1,0:T(8,128)(2,1)} %copy-done.46), kind=kOutput, calls=%fused_computation.75 | convolution fusion | flops 3984588800 | bytes 15581184 | tf_op jit(solution)/shard_map/td,tf->df/dot_general | solution.py:202
  386.7 10.4 %pad_maximum_fusion = f32[2,512,3200]{2,1,0:T(8,128)} fusion(f32[1,512,3200]{2,1,0:T(8,128)} %convolution_bitcast_fusion, f32[1,512,3200]{2,1,0:T(8,128)} %convolution_bitcast_fusion.1), kind=kLoop, calls=%fused_computation.74 | loop fusion | flops 3276800 | bytes 26214400 | tf_op jit(solution)/shard_map/stack | solution.py:269
  399.1 2.2 select_bitcast_fusion.5
  401.6 4.9 fusion.57
  410.7 39.5 %psum.7 = f32[14464]{0:T(1024)S(1)} all-reduce(f32[14464]{0:T(1024)S(1)} %constant_dynamic-update-slice_fusion), channel_id=1, replica_groups=mesh['dp'=8,'cam'=4] {'dp','cam'}, use_global_device_ids=true, to_apply=%region_26.27 | all-reduce | flops 14464 | bytes 115712 | tf_op jit(solution)/shard_map/psum | solution.py:267
  451.7 2.3 collective-permute-start.3
  456.1 12.9 %collective-permute-done.3 = bf16[2,1,304,512]{3,2,0,1:T(8,128)(2,1)S(1)} collective-permute-done((bf16[2,1,304,512]{3,2,0,1:T(8,128)(2,1)S(1)}, bf16[2,1,304,512]{3,2,0,1:T(8,128)(2,1)S(1)}, u32[]{:S(2)}, u32[]{:S(2)}) %collective-permute-start.3) | collective-permute-done | bytes 622624 | tf_op jit(solution)/shard_map/ppermute | solution.py:27
  470.2 13.0 %collective-permute-done.5 = bf16[2,1,304,512]{3,2,0,1:T(8,128)(2,1)S(1)} collective-permute-done((bf16[2,1,304,512]{3,2,0,1:T(8,128)(2,1)S(1)}, bf16[2,1,304,512]{3,2,0,1:T(8,128)(2,1)S(1)}, u32[]{:S(2)}, u32[]{:S(2)}) %collective-permute-start.5) | collective-permute-done | bytes 622624 | tf_op jit(solution)/shard_map/ppermute | solution.py:27
  485.5 32.3 %all-reduce.3.cloned.1.call-done = f32[4,512,512]{2,0,1:T(4,128)} async-done(((f32[4,512,512]{2,0,1:T(4,128)}), f32[4,512,512]{2,0,1:T(4,128)}) %all-reduce.3.cloned.1.call-update) | async-done | bytes 4194320
  519.6 157.0 %reduce-scatter.2.cloned.1.call-done = f32[2,16,3200]{2,1,0:T(8,128)} async-done(((f32[2,512,3200]{2,1,0:T(8,128)}), f32[2,16,3200]{2,1,0:T(8,128)}) %reduce-scatter.2.cloned.1.call-update) | async-done | bytes 409616 | tf_op jit(solution)/shard_map/reduce_scatter | solution.py:272
  676.6 2.4 multiply_add_fusion.2
  (256 shorter events, 132.5 us)
Async XLA Ops:
  7.2 64.6 %all-gather.3.cloned.1.call-start = ((), (), s32[]{:S(2)}) async-start(), calls=%async_computation.1 | async-start | bytes 2162688 | tf_op jit(solution)/shard_map/all_gather | solution.py:147
  8.8 144.7 %all-gather.5.cloned.1.call-start = ((), (), s32[]{:S(2)}) async-start(), calls=%async_computation.2 | async-start | bytes 6758400 | tf_op jit(solution)/shard_map/all_gather | solution.py:148
  11.9 3.4 collective-permute-start
  16.8 1.0 copy-start.10
  16.8 1.4 copy-start.11
  16.8 4.3 copy-start.21
  16.8 5.1 slice-start.1
  16.8 5.1 copy-start.29
  18.2 32.8 %collective-permute-start.1 = (bf16[2,2,1,304,512]{4,3,1,0,2:T(8,128)(2,1)S(1)}, bf16[2,2,1,304,512]{4,3,1,0,2:T(8,128)(2,1)S(1)}, u32[]{:S(2)}, u32[]{:S(2)}) collective-permute-start(bf16[2,2,1,304,512]{4,3,1,0,2:T(8,128)(2,1)S(1)} %fusion.76), channel_id=1, source_target_pairs={{0,2},{1,3},{2,0},{3,1},{4,6},{5,7},{6,4},{7,5},{8,10},{9,11},{10,... | collective-permute-start | bytes 3735560 | tf_op jit(solution)/shard_map/ppermute | solution.py:27
  21.8 495.9 %all-reduce.3.cloned.1.call-start = ((), (), s32[]{:S(2)}) async-start(), calls=%async_computation.4 | async-start | bytes 8388608
  22.5 31.9 %copy-start.39 = (f32[512]{0:T(512)}, f32[512]{0:T(512)S(1)}, u32[]{:S(2)}) copy-start(f32[512]{0:T(512)S(1)} %get-tuple-element.275) | copy-start | bytes 6148
  53.9 1.4 copy-start
  57.9 17.3 %copy-start.4 = (f32[1216,512]{1,0:T(8,128)}, f32[1216,512]{1,0:T(8,128)S(1)}, u32[]{:S(2)}) copy-start(f32[1216,512]{1,0:T(8,128)S(1)} %scatter-add.4) | copy-start | bytes 7471108
  82.2 3.8 copy-start.20
  147.6 1.5 copy-start.6
  152.3 1.1 slice-start
  152.8 0.6 copy-start.34
  153.5 42.4 %copy-start.44 = (f32[512]{0:T(512)S(1)}, f32[512]{0:T(512)}, u32[]{:S(2)}) copy-start(f32[512]{0:T(512)} %get-tuple-element.276) | copy-start | bytes 6148
  153.5 42.4 %copy-start.45 = (bf16[2,512,3200]{2,1,0:T(8,128)(2,1)S(1)}, bf16[2,512,3200]{2,1,0:T(8,128)(2,1)}, u32[]{:S(2)}) copy-start(bf16[2,512,3200]{2,1,0:T(8,128)(2,1)} %all-gather.5.cloned.1.call-done) | copy-start | bytes 19660804
  195.9 5.0 copy-start.46
  195.9 5.5 copy-start.15
  200.9 1.7 copy-start.1
  202.6 1.6 copy-start.40
  202.6 1.6 copy-start.43
  231.0 10.4 %copy-start.3 = (f32[1216,512]{1,0:T(8,128)S(1)}, f32[1216,512]{1,0:T(8,128)}, u32[]{:S(2)}) copy-start(f32[1216,512]{1,0:T(8,128)} %get-tuple-element.269) | copy-start | bytes 7471108
  231.0 10.4 %copy-start.7 = (bf16[1216,3200]{1,0:T(8,128)(2,1)S(1)}, bf16[1216,3200]{1,0:T(8,128)(2,1)}, u32[]{:S(2)}) copy-start(bf16[1216,3200]{1,0:T(8,128)(2,1)} %get-tuple-element.290) | copy-start | bytes 23347204
  241.4 7.2 %copy-start.35 = (f32[1216]{0:T(1024)S(1)}, f32[1216]{0:T(1024)}, u32[]{:S(2)}) copy-start(f32[1216]{0:T(1024)} %copy-done.34) | copy-start | bytes 14596
  249.5 4.1 copy-start.13
  249.5 2.2 copy-start.19
  354.9 2.9 copy-start.8
  357.8 5.1 copy-start.5
  362.9 4.4 copy-start.24
  375.2 1.3 copy-start.23
  375.2 301.3 %reduce-scatter.2.cloned.1.call-start = ((), (), s32[]{:S(2)}) async-start(), calls=%async_computation.3 | async-start | bytes 13516800 | tf_op jit(solution)/shard_map/reduce_scatter | solution.py:272
  397.1 1.8 copy-start.2
  397.2 4.5 copy-start.14
  401.3 48.9 %collective-permute-start.2 = (bf16[2,1,304,512]{3,2,0,1:T(8,128)(2,1)}, bf16[2,1,304,512]{3,2,0,1:T(8,128)(2,1)}, u32[]{:S(2)}, u32[]{:S(2)}) collective-permute-start(bf16[2,1,304,512]{3,2,0,1:T(8,128)(2,1)} %select_bitcast_fusion.5), channel_id=1, source_target_pairs={{0,1},{1,0},{2,3},{3,2},{4,5},{5,4},{6,7},{7,6},{8,9},{9,8},{10,11... | collective-permute-start | bytes 1867784 | tf_op jit(solution)/shard_map/ppermute | solution.py:27
  401.6 8.6 %copy-start.18 = (bf16[8,1,1216,64]{2,3,1,0:T(8,128)(2,1)S(1)}, bf16[8,1,1216,64]{2,3,1,0:T(8,128)(2,1)}, u32[]{:S(2)}) copy-start(bf16[8,1,1216,64]{2,3,1,0:T(8,128)(2,1)} %get-tuple-element.112) | copy-start | bytes 3735556
  406.6 1.5 copy-start.16
  406.6 2.6 copy-start.9
  406.6 4.0 copy-start.42
  406.6 4.0 copy-start.41
  406.6 43.6 %copy-start.12 = (bf16[1216,512]{1,0:T(8,128)(2,1)S(1)}, bf16[1216,512]{1,0:T(8,128)(2,1)}, u32[]{:S(2)}) copy-start(bf16[1216,512]{1,0:T(8,128)(2,1)} %get-tuple-element.270) | copy-start | bytes 3735556
  409.0 45.0 %collective-permute-start.4 = (bf16[2,1,304,512]{3,2,0,1:T(8,128)(2,1)}, bf16[2,1,304,512]{3,2,0,1:T(8,128)(2,1)S(1)}, u32[]{:S(2)}, u32[]{:S(2)}) collective-permute-start(bf16[2,1,304,512]{3,2,0,1:T(8,128)(2,1)} %fusion.82), channel_id=1, source_target_pairs={{0,1},{1,0},{2,3},{3,2},{4,5},{5,4},{6,7},{7,6},{8,9},{9,8},{10,11... | collective-permute-start | bytes 1867784 | tf_op jit(solution)/shard_map/ppermute | solution.py:27
  450.2 3.8 copy-start.17
  451.7 17.3 %collective-permute-start.3 = (bf16[2,1,304,512]{3,2,0,1:T(8,128)(2,1)S(1)}, bf16[2,1,304,512]{3,2,0,1:T(8,128)(2,1)S(1)}, u32[]{:S(2)}, u32[]{:S(2)}) collective-permute-start(bf16[2,1,304,512]{3,2,0,1:T(8,128)(2,1)S(1)} %select_bitcast_fusion.4), channel_id=1, source_target_pairs={{0,2},{1,3},{2,0},{3,1},{4,6},{5,7},{6,4},{7,5},{8,10},{9,11},{10,... | collective-permute-start | bytes 1867784 | tf_op jit(solution)/shard_map/ppermute | solution.py:27
  454.4 0.8 copy-start.30
  454.4 0.9 copy-start.36
  454.5 0.9 copy-start.37
  454.5 0.9 copy-start.38
  454.7 28.6 %collective-permute-start.5 = (bf16[2,1,304,512]{3,2,0,1:T(8,128)(2,1)S(1)}, bf16[2,1,304,512]{3,2,0,1:T(8,128)(2,1)S(1)}, u32[]{:S(2)}, u32[]{:S(2)}) collective-permute-start(bf16[2,1,304,512]{3,2,0,1:T(8,128)(2,1)S(1)} %fusion.83), channel_id=1, source_target_pairs={{0,2},{1,3},{2,0},{3,1},{4,6},{5,7},{6,4},{7,5},{8,10},{9,11},{10,... | collective-permute-start | bytes 1867784 | tf_op jit(solution)/shard_map/ppermute | solution.py:27
  483.6 35.0 %copy-start.25 = (f32[4,16,512]{2,1,0:T(8,128)S(1)}, f32[4,16,512]{2,1,0:T(8,128)}, u32[]{:S(2)}) copy-start(f32[4,16,512]{2,1,0:T(8,128)} %param.26) | copy-start | bytes 393220
  483.7 35.0 %copy-start.31 = (f32[4,16,512]{2,1,0:T(8,128)S(1)}, f32[4,16,512]{2,1,0:T(8,128)}, u32[]{:S(2)}) copy-start(f32[4,16,512]{2,1,0:T(8,128)} %param.29) | copy-start | bytes 393220
  483.7 35.0 %copy-start.32 = (f32[4,16,512]{2,1,0:T(8,128)S(1)}, f32[4,16,512]{2,1,0:T(8,128)}, u32[]{:S(2)}) copy-start(f32[4,16,512]{2,1,0:T(8,128)} %param.27) | copy-start | bytes 393220
  483.7 35.0 %copy-start.33 = (f32[4,16,512]{2,1,0:T(8,128)S(1)}, f32[4,16,512]{2,1,0:T(8,128)}, u32[]{:S(2)}) copy-start(f32[4,16,512]{2,1,0:T(8,128)} %param.28) | copy-start | bytes 393220
  483.7 192.9 %copy-start.22 = (f32[2,16,3200]{2,1,0:T(8,128)S(1)}, f32[2,16,3200]{2,1,0:T(8,128)}, u32[]{:S(2)}) copy-start(f32[2,16,3200]{2,1,0:T(8,128)} %param.30) | copy-start | bytes 1228804
  483.7 192.8 %copy-start.26 = (f32[2,16,3200]{2,1,0:T(8,128)S(1)}, f32[2,16,3200]{2,1,0:T(8,128)}, u32[]{:S(2)}) copy-start(f32[2,16,3200]{2,1,0:T(8,128)} %param.33) | copy-start | bytes 1228804
  483.7 192.8 %copy-start.27 = (f32[2,16,3200]{2,1,0:T(8,128)S(1)}, f32[2,16,3200]{2,1,0:T(8,128)}, u32[]{:S(2)}) copy-start(f32[2,16,3200]{2,1,0:T(8,128)} %param.31) | copy-start | bytes 1228804
  483.7 192.8 %copy-start.28 = (f32[2,16,3200]{2,1,0:T(8,128)S(1)}, f32[2,16,3200]{2,1,0:T(8,128)}, u32[]{:S(2)}) copy-start(f32[2,16,3200]{2,1,0:T(8,128)} %param.32) | copy-start | bytes 1228804
Sparse Core Ops, SparseCore 0:
  11.5 60.1 all-gather.2
  75.2 69.5 all-gather.4
  375.3 142.3 all-reduce.2
  519.9 156.6 reduce-scatter.1
where the time goes:
time: 697 us; the launch traced here: 686 us
  waiting for transfers between devices  260 us (37%)
  matrix products  237 us (34%)
  other arithmetic  69.3 us (10%)
  local copies, waits for them, and re-layouts  57.7 us (8%)
  blocking collectives  39.5 us (6%)
  between operations  15.1 us (2%)
    reduce_scatter x1, waiting for transfers between devices, local(): lax.psum_scatter(ffn_grad, ('dp', 'cam'), scatter_dimension=1, tiled=True)  157 us
    ppermute x6, waiting for transfers between devices, partner(): return lax.ppermute(value, axis, pairs)  57.2 us
    dot_general x1, matrix products, local(): jnp.dot(normed_low, ffn_full[0], preferred_element_type=jnp.float32)  42.4 us
    psum x1, blocking collectives, local(): small_total = lax.psum(small_grad, ('dp', 'cam'))  39.5 us
    dot_general x16, matrix products, head_scores(): jnp.einsum('iqd,ikd->iqk', query_head, key_head, preferred_element_type=j...  36.4 us
    unnamed x5, waiting for transfers between devices  32.3 us
    dot_general x8, matrix products, attend_head(): jnp.einsum('iqk,ikd->iqd', probs_low, value_head, preferred_element_type=...  21.9 us
    dot_general x8, matrix products, attend_back(): jnp.einsum('iqk,iqd->ikd', score_grad, query_head, preferred_element_type...  21.3 us
  transfers between devices with their start and end apart: 10, of which 7 were waited for; matrix products, arithmetic and copies ran while one was open for 19% of the time, Pallas kernels for 0%

commit v1 on v0

v1 whole, which is shorter than its diff:
```python
import functools

import jax
import jax.numpy as jnp
from jax import lax
from jax.experimental import pallas as pl
from jax.experimental.pallas import tpu as pltpu
from jax.sharding import PartitionSpec as P

D = 512
HEADS = 8
NJ = 14
ADAM_STEP = 10
HD = 64
PAIR = 2 * HD
PAIRS = HEADS // 2
GROUPS = 2
GROUP_PAIRS = PAIRS // GROUPS
GROUP_COLS = GROUP_PAIRS * PAIR
BLOCKS = 32
ROWS = D // BLOCKS
HALF = BLOCKS // 2
CHUNK = 640

norm_eps = 1e-05
beta_first = 0.5
beta_second = 0.5
adam_eps = 1e-08
rate_matrix = 0.02
rate_small = 0.05
decay_matrix = 0.1
ema_decay = 0.75
log2e = 1.4426950408889634
score_scale = HD**-0.5
F32 = jnp.float32
BF16 = jnp.bfloat16
VMEM_LIMIT = 60 * 2**20


def adam_update(master, grad_total, first_old, second_old, average_old, rate, decay):
    first_new = beta_first * first_old + (1.0 - beta_first) * grad_total
    second_new = beta_second * second_old + (1.0 - beta_second) * grad_total * grad_total
    first_hat = first_new / (1.0 - beta_first**ADAM_STEP)
    second_hat = second_new / (1.0 - beta_second**ADAM_STEP)
    master_new = master - rate * (first_hat / (jnp.sqrt(second_hat) + adam_eps) + decay * master)
    average_new = ema_decay * average_old + (1.0 - ema_decay) * master_new
    return (master_new, first_new, second_new, average_new)


def dot(left, right, left_dim, right_dim):
    return lax.dot_general(
        left, right, (((left_dim,), (right_dim,)), ((), ())), preferred_element_type=F32
    )


def apart(position, order, core):
    outer, inner, depth = position // 8, position // 4 % 2, position % 4
    x_bit, y_bit = (outer, inner) if order == "xy" else (inner, outer)
    return depth * 8 + y_bit * 4 + x_bit * 2 + core


def row_blocks(device, order):
    for core in range(2):
        for position in range(HALF):
            start = (device ^ apart(position, order, core)) * ROWS
            yield core, position, pl.ds(pl.multiple_of(start, ROWS), ROWS)


def put_rows(target, sides, order, device, part=None):
    for core, position, rows in row_blocks(device, order):
        block = sides[core].at[position] if part is None else sides[core].at[position, part]
        target[rows, :] = block[...]


def take_rows(source, sides, order, device):
    for core, position, rows in row_blocks(device, order):
        sides[core][position] = source[rows, :].astype(BF16)


def mean_last(values):
    return jnp.sum(values, axis=-1, keepdims=True) * (1.0 / D)


def normal_rows(values):
    centred = values - mean_last(values)
    inverse = lax.rsqrt(mean_last(centred * centred) + norm_eps)
    return centred * inverse, inverse


def normal_back(normal, inverse, grad):
    return inverse * (grad - mean_last(grad) - normal * mean_last(grad * normal))


def column_sum(values):
    return jnp.sum(values, axis=0, keepdims=True)


def spread_heads(values, other):
    lane = lax.broadcasted_iota(jnp.int32, (1, PAIR), 1)
    low = lane < HD
    return jnp.where(low, values, other), jnp.where(low, other, values)


def attend_kernel(first, seg_len, where, *refs):
    if first:
        pieces, joint, refs = refs[:4], refs[4], refs[5:]
    else:
        rounded, refs = refs[0], refs[1:]
    qk_sides, vo_sides, bias_q, bias_v, refs = refs[:2], refs[2:4], refs[4], refs[5], refs[6:]
    if first:
        rounded, top_rows, refs = refs[0], refs[1], refs[2:]
    q_out, k_out, v_out, a_out, l_out, weight, logs = refs
    device, slot = where[0], where[1]

    if first:

        @pl.when(pl.program_id(0) == 0)
        def _():
            for k in range(4):
                start = pl.multiple_of((slot ^ k) * seg_len, 16)
                rounded[pl.ds(start, seg_len), :] = pieces[k][...]
            top = rounded[:16, :].astype(F32)
            at = lax.broadcasted_iota(jnp.int32, (16, 1), 0)
            top = jnp.where(at == 1, top + joint[...], top)
            top_rows[...] = top[:8]
            rounded[:16, :] = top.astype(BF16)

    put_rows(weight.at[:, :PAIR], qk_sides, "xy", device, 0)
    put_rows(weight.at[:, PAIR : 2 * PAIR], qk_sides, "xy", device, 1)
    put_rows(weight.at[:, 2 * PAIR :], vo_sides, "yx", device, 0)
    projected = dot(rounded[...], weight[...], 1, 0)
    q_out[...] = (projected[:, :PAIR] + bias_q[...]).astype(BF16)
    keys = projected[:, PAIR : 2 * PAIR].astype(BF16)
    values = (projected[:, 2 * PAIR :] + bias_v[...]).astype(BF16)
    k_out[...] = keys
    v_out[...] = values
    lane = lax.broadcasted_iota(jnp.int32, (1, PAIR), 1)
    low = lane < HD
    value_heads = spread_heads(values, jnp.ones_like(values))
    scale = log2e * score_scale
    for step in range(4):
        rows = pl.ds(step * seg_len, seg_len)
        query = q_out[rows, :]
        mixed, tops = [], []
        for query_head, value_head in zip(spread_heads(query, jnp.zeros_like(query)), value_heads):
            scores = dot(query_head, keys, 1, 1)
            top = jnp.max(scores, axis=1, keepdims=True) * scale
            probs = jnp.exp2(scores * scale - top).astype(BF16)
            mixed.append(dot(probs, value_head, 1, 0))
            tops.append(top)
        total = pltpu.roll(jnp.where(low, mixed[1], mixed[0]), HD, 1)
        a_out[rows, :] = (jnp.where(low, mixed[0], mixed[1]) / total).astype(BF16)
        logs[rows, :] = jnp.where(low, tops[0], tops[1]) + jnp.log2(total)
    turned = logs[...].T
    l_out[0:1, :] = turned[0:1]
    l_out[1:2, :] = turned[HD : HD + 1]


def gate_both(values):
    size = jnp.abs(values)
    fraction = 1.0 / (1.0 + (0.3275911 * 0.5**0.5) * size)
    bell = jnp.exp2(values * values * (-0.5 * log2e))
    series = 0.5 * 1.061405429 * fraction - 0.5 * 1.453152027
    series = series * fraction + 0.5 * 1.421413741
    series = series * fraction - 0.5 * 0.284496736
    series = series * fraction + 0.5 * 0.254829592
    tail = series * fraction * bell
    below = jnp.where(values > 0.0, 1.0 - tail, tail)
    return values * below, below + values * bell * 0.3989422804014327


def forward_kernel(seg_len, where, *refs):
    rounded, top_rows, refs = refs[0], refs[1], refs[2:]
    mixed, refs = refs[:GROUPS], refs[GROUPS:]
    vo_sides, up_sides, down_sides, refs = refs[:2], refs[2:4], refs[4:6], refs[6:]
    vectors, hidden_bias, cotangents, refs = refs[0], refs[1], refs[2:6], refs[6:]
    h1_out, y1_out, g_out, slope_out, pieces, refs = refs[0], refs[1], refs[2], refs[3], refs[4:8], refs[8:]
    dh2_out, vector_grads, normed, total, w_out, w_up, w_down = refs
    device, slot = where[0], where[1]
    seq_len = 4 * seg_len
    out_scale = (seq_len / 3.0) ** 0.5
    chunk = pl.program_id(0)

    @pl.when(chunk == 0)
    def _():
        put_rows(w_out, vo_sides, "yx", device, 1)
        for step in range(4):
            rows = pl.ds(step * seg_len, seg_len)
            summed = rounded[rows, :].astype(F32)
            if step == 0:
                summed = jnp.concatenate([top_rows[...], summed[8:]], axis=0)
            branch = sum(
                dot(mixed[g][rows, :], w_out[g * GROUP_COLS : (g + 1) * GROUP_COLS, :], 1, 0)
                for g in range(GROUPS)
            )
            summed = summed + (branch * out_scale + vectors[2:3, :])
            h1_out[rows, :] = summed
            normal, _ = normal_rows(summed)
            result = normal * vectors[3:4, :] + vectors[4:5, :]
            normed[rows, :] = result
            y1_out[rows, :] = result.astype(BF16)
        total[...] = jnp.zeros_like(total)

    put_rows(w_up, up_sides, "xy", device)
    put_rows(w_down, down_sides, "yx", device)
    for step in range(4):
        rows = pl.ds(step * seg_len, seg_len)
        inner = dot(y1_out[rows, :], w_up[...], 1, 0) + hidden_bias[...]
        active, slope = gate_both(inner)
        active = active.astype(BF16)
        g_out[rows, :] = active
        slope_out[rows, :] = slope.astype(BF16)
        total[rows, :] += dot(active, w_down[...], 1, 1)

    @pl.when(chunk == pl.num_programs(0) - 1)
    def _():
        gain_grad = shift_grad = bias_grad = 0.0
        for k in range(4):
            rows = pl.ds(pl.multiple_of((slot ^ k) * seg_len, 16), seg_len)
            normal, inverse = normal_rows(normed[rows, :] + (total[rows, :] + vectors[5:6, :]))
            pieces[k][...] = (normal * vectors[6:7, :] + vectors[7:8, :]).astype(BF16)
            cotangent = cotangents[k][...].astype(F32)
            gain_grad += column_sum(cotangent * normal)
            shift_grad += column_sum(cotangent)
            middle = normal_back(normal, inverse, cotangent * vectors[6:7, :])
            dh2_out[rows, :] = middle
            bias_grad += column_sum(middle.astype(BF16).astype(F32))
        vector_grads[0:1, :] = gain_grad
        vector_grads[1:2, :] = shift_grad
        vector_grads[2:3, :] = bias_grad


def backward_kernel(seg_len, where, *refs):
    dh2, h1, y1, active, slope, refs = refs[0], refs[1], refs[2], refs[3], refs[4], refs[5:]
    mixed, refs = refs[:GROUPS], refs[GROUPS:]
    vo_sides, up_sides, down_sides, vectors, refs = refs[:2], refs[2:4], refs[4:6], refs[6], refs[7:]
    up_grads, down_grads, out_grads, refs = refs[:2], refs[2:4], refs[4:6], refs[6:]
    hidden_grad, dh1_out, da_out, vector_grads, refs = refs[0], refs[1], refs[2], refs[3], refs[4:]
    y1_turned, df_turned, df, dz, total, w_out, w_up, w_down, grad = refs
    device = where[0]
    seq_len = 4 * seg_len
    out_scale = (seq_len / 3.0) ** 0.5
    chunk = pl.program_id(0)

    @pl.when(chunk == 0)
    def _():
        rounded = dh2[...].astype(BF16)
        df[...] = rounded
        df_turned[...] = rounded.T
        y1_turned[...] = y1[...].T
        total[...] = dh2[...]

    put_rows(w_up, up_sides, "xy", device)
    put_rows(w_down, down_sides, "yx", device)
    bias_grad = 0.0
    for step in range(4):
        rows = pl.ds(step * seg_len, seg_len)
        inner = (dot(df[rows, :], w_down[...], 1, 0) * slope[rows, :].astype(F32)).astype(BF16)
        dz[rows, :] = inner
        bias_grad += column_sum(inner.astype(F32))
        total[rows, :] += dot(inner, w_up[...], 1, 1)
    hidden_grad[...] = bias_grad
    grad[...] = dot(df_turned[...], active[...], 1, 0)
    take_rows(grad, down_grads, "yx", device)
    grad[...] = dot(y1_turned[...], dz[...], 1, 0)
    take_rows(grad, up_grads, "xy", device)

    @pl.when(chunk == pl.num_programs(0) - 1)
    def _():
        put_rows(w_out, vo_sides, "yx", device, 1)
        gain_grad = shift_grad = bias_grad = 0.0
        for step in range(4):
            rows = pl.ds(step * seg_len, seg_len)
            normal, inverse = normal_rows(h1[rows, :])
            above = total[rows, :]
            gain_grad += column_sum(above * normal)
            shift_grad += column_sum(above)
            summed = normal_back(normal, inverse, above * vectors[3:4, :])
            dh1_out[rows, :] = summed
            rounded = summed.astype(BF16)
            df[rows, :] = rounded
            bias_grad += column_sum(rounded.astype(F32))
            da_out[rows, :] = (dot(rounded, w_out[...], 1, 1) * out_scale).astype(BF16)
        vector_grads[0:1, :] = gain_grad
        vector_grads[1:2, :] = shift_grad
        vector_grads[2:3, :] = bias_grad
        for g in range(GROUPS):
            cols = pl.ds(g * GROUP_COLS, GROUP_COLS)
            grad[cols, :D] = dot(mixed[g][...], df[...], 0, 0) * out_scale
        take_rows(grad.at[:, :D], out_grads, "yx", device)


def attend_back_kernel(last, seg_len, where, *refs):
    q, k, v, a, da, logs, rounded, before, refs = *refs[:8], refs[8:]
    qk_sides, vo_sides, refs = refs[:2], refs[2:4], refs[4:]
    sides, refs = refs[: 2 * GROUP_PAIRS], refs[2 * GROUP_PAIRS :]
    bias_grads, refs = refs[0], refs[1:]
    if last:
        own, sends, top_rows, total, refs = refs[0], refs[1:4], refs[4], refs[5], refs[6:]
    else:
        total, refs = refs[0], refs[1:]
    turned, weight, parts, query_turned, grad = refs
    device, slot = where[0], where[1]
    seq_len = 4 * seg_len
    pair = pl.program_id(0)

    @pl.when(pair == 0)
    def _():
        turned[...] = rounded[...].T
        total[...] = before[...]

    put_rows(weight.at[:, :PAIR], qk_sides, "xy", device, 0)
    put_rows(weight.at[:, PAIR : 2 * PAIR], qk_sides, "xy", device, 1)
    put_rows(weight.at[:, 2 * PAIR :], vo_sides, "yx", device, 0)

    queries, mixed_grads = q[...], da[...]
    zeros = jnp.zeros_like(queries)
    query_heads = spread_heads(queries, zeros)
    grad_heads = spread_heads(mixed_grads, zeros)
    product = (mixed_grads.astype(F32) * a[...].astype(F32)).T
    inner = (column_sum(product[:HD]), column_sum(product[HD:]))
    start = 0
    while start < seq_len:
        size = min(256, seq_len - start)
        rows = pl.ds(start, size)
        none = jnp.zeros((size, PAIR), BF16)
        key_grad = value_grad = query_grad = 0.0
        heads = zip(spread_heads(k[rows, :], none), spread_heads(v[rows, :], none))
        for h, (key_head, value_head) in enumerate(heads):
            scores = dot(key_head, queries, 1, 1)
            probs = jnp.exp2(scores * (log2e * score_scale) - logs[h : h + 1, :])
            grads = (probs * (dot(value_head, mixed_grads, 1, 1) - inner[h])).astype(BF16)
            value_grad += dot(probs.astype(BF16), grad_heads[h], 1, 0)
            key_grad += dot(grads, query_heads[h], 1, 0)
            query_grad += dot(key_head, grads, 0, 0)
        parts[rows, PAIR : 2 * PAIR] = (key_grad * score_scale).astype(BF16)
        parts[rows, 2 * PAIR :] = value_grad.astype(BF16)
        if start == 0:
            query_turned[...] = query_grad
        else:
            query_turned[...] += query_grad
        start += size
    parts[:, :PAIR] = (query_turned[...].T * score_scale).astype(BF16)
    bias_grads[0:1, :] = column_sum(parts[:, :PAIR].astype(F32))
    bias_grads[1:2, :] = column_sum(parts[:, 2 * PAIR :].astype(F32))
    total[...] += dot(parts[...], weight[...], 1, 1)
    grad[...] = dot(turned[...], parts[...], 1, 0)
    for n in range(GROUP_PAIRS):

        @pl.when(pair == n)
        def _(n=n):
            take_rows(grad, sides[2 * n : 2 * n + 2], pair_order(n), device)

    if last:

        @pl.when(pair == pl.num_programs(0) - 1)
        def _():
            top_rows[...] = total[:8, :]
            for n in range(4):
                piece = total[pl.ds(pl.multiple_of((slot ^ n) * seg_len, 16), seg_len), :]
                if n == 0:
                    own[...] = piece
                else:
                    sends[n - 1][...] = piece.astype(BF16)


def pair_order(pair):
    return "yx" if pair % 2 else "xy"


def call(kernel, name, where, grid, operands, results, scratch, flops, exps=0):
    def spec(block, index):
        return pl.BlockSpec(block, lambda i, _: index(i))

    moved = sum(x.size * x.dtype.itemsize for x, _, _ in (*operands, *results))
    return pl.pallas_call(
        kernel,
        grid_spec=pltpu.PrefetchScalarGridSpec(
            num_scalar_prefetch=1,
            grid=(grid,),
            in_specs=[spec(block, index) for _, block, index in operands],
            out_specs=[spec(block, index) for _, block, index in results],
            scratch_shapes=[pltpu.VMEM(shape, kind) for shape, kind in scratch],
        ),
        out_shape=[shape for shape, _, _ in results],
        compiler_params=pltpu.CompilerParams(vmem_limit_bytes=VMEM_LIMIT),
        cost_estimate=pl.CostEstimate(flops=flops, bytes_accessed=moved, transcendentals=exps),
        name=name,
    )(where, *(x for x, _, _ in operands))


def whole(x):
    return (x, x.shape, lambda i: (0,) * len(x.shape))


def shape_of(shape, kind):
    return jax.ShapeDtypeStruct(shape, kind)


def whole_out(shape, kind):
    return whole(shape_of(shape, kind))


def attend(group, where, source, sides, vectors, seg_len):
    seq_len = 4 * seg_len
    first = group == 0
    base = group * GROUP_PAIRS

    def at(i):
        return (0, i + base)

    operands = [whole(x) for x in source]
    operands += [(x, (HALF, 2, ROWS, PAIR), lambda i: (0, 0, 0, i + base)) for x in sides]
    operands += [(vectors[n : n + 1], (1, PAIR), at) for n in range(2)]
    results = []
    if first:
        results += [whole_out((seq_len, D), BF16), whole_out((8, D), F32)]
    columns = (shape_of((seq_len, GROUP_COLS), BF16), (seq_len, PAIR), lambda i: (0, i))
    results += [columns] * 4
    results += [(shape_of((GROUP_PAIRS, 2, seq_len), F32), (None, 2, seq_len), lambda i: (i, 0, 0))]
    scratch = [((D, 3 * PAIR), BF16), ((seq_len, PAIR), F32)]
    scores = seq_len * seq_len * 2 * GROUP_PAIRS
    return call(
        functools.partial(attend_kernel, first, seg_len),
        f"attend_{group}",
        where,
        GROUP_PAIRS,
        operands,
        results,
        scratch,
        scores * 16 * HD,
        scores,
    )


def feed_forward(where, rounded, top_rows, mixed, vo, up, down, vectors, hidden_bias, cotangents):
    seq_len = rounded.shape[0]
    seg_len = seq_len // 4
    hidden = up[0].shape[-1]
    operands = [whole(x) for x in (rounded, top_rows, *mixed, *vo)]
    operands += [(x, (HALF, ROWS, CHUNK), lambda i: (0, 0, i)) for x in (*up, *down)]
    operands += [whole(vectors), (hidden_bias, (1, CHUNK), lambda i: (0, i))]
    operands += [whole(x) for x in cotangents]
    wide = (shape_of((seq_len, hidden), BF16), (seq_len, CHUNK), lambda i: (0, i))
    results = [whole_out((seq_len, D), F32), whole_out((seq_len, D), BF16), wide, wide]
    results += [whole_out((seg_len, D), BF16)] * 4
    results += [whole_out((seq_len, D), F32), whole_out((8, D), F32)]
    scratch = [((seq_len, D), F32), ((seq_len, D), F32), ((D, D), BF16)]
    scratch += [((D, CHUNK), BF16)] * 2
    return call(
        functools.partial(forward_kernel, seg_len),
        "feed_forward",
        where,
        hidden // CHUNK,
        operands,
        results,
        scratch,
        seq_len * D * (D + 2 * hidden) * 2,
        2 * seq_len * hidden,
    )


def feed_back(where, dh2, h1, y1, active, slope, mixed, vo, up, down, vectors):
    seq_len = dh2.shape[0]
    seg_len = seq_len // 4
    hidden = up[0].shape[-1]
    operands = [whole(x) for x in (dh2, h1, y1)]
    operands += [(x, (seq_len, CHUNK), lambda i: (0, i)) for x in (active, slope)]
    operands += [whole(x) for x in (*mixed, *vo)]
    operands += [(x, (HALF, ROWS, CHUNK), lambda i: (0, 0, i)) for x in (*up, *down)]
    operands += [whole(vectors)]
    wide = (shape_of((HALF, ROWS, hidden), BF16), (HALF, ROWS, CHUNK), lambda i: (0, 0, i))
    results = [wide] * 4 + [whole_out((HALF, ROWS, D), BF16)] * 2
    results += [(shape_of((1, hidden), F32), (1, CHUNK), lambda i: (0, i))]
    results += [whole_out((seq_len, D), F32), whole_out((seq_len, D), BF16), whole_out((8, D), F32)]
    scratch = [((D, seq_len), BF16)] * 2 + [((seq_len, D), BF16), ((seq_len, CHUNK), BF16)]
    scratch += [((seq_len, D), F32), ((D, D), BF16)] + [((D, CHUNK), BF16)] * 2 + [((D, CHUNK), F32)]
    return call(
        functools.partial(backward_kernel, seg_len),
        "feed_back",
        where,
        hidden // CHUNK,
        operands,
        results,
        scratch,
        seq_len * D * (2 * D + 4 * hidden) * 2,
    )


def attend_back(group, where, heads, da, logs, rounded, before, sides, seg_len):
    seq_len = 4 * seg_len
    last = group == GROUPS - 1
    base = group * GROUP_PAIRS
    operands = [(x, (seq_len, PAIR), lambda i: (0, i)) for x in heads]
    operands += [(da, (seq_len, PAIR), lambda i: (0, i + base))]
    operands += [(logs, (None, 2, seq_len), lambda i: (i, 0, 0)), whole(rounded), whole(before)]
    operands += [(x, (HALF, 2, ROWS, PAIR), lambda i: (0, 0, 0, i + base)) for x in sides]
    results = [whole_out((HALF, ROWS, 3 * PAIR), BF16)] * (2 * GROUP_PAIRS)
    results += [(shape_of((8, GROUP_COLS), F32), (8, PAIR), lambda i: (0, i))]
    scratch = []
    if last:
        results += [whole_out((seg_len, D), F32)] + [whole_out((seg_len, D), BF16)] * 3
        results += [whole_out((8, D), F32)]
        scratch += [((seq_len, D), F32)]
    else:
        results += [whole_out((seq_len, D), F32)]
    scratch += [((D, seq_len), BF16), ((D, 3 * PAIR), BF16), ((seq_len, 3 * PAIR), BF16)]
    scratch += [((PAIR, seq_len), F32), ((D, 3 * PAIR), F32)]
    scores = seq_len * seq_len * 2 * GROUP_PAIRS
    return call(
        functools.partial(attend_back_kernel, last, seg_len),
        f"attend_back_{group}",
        where,
        GROUP_PAIRS,
        operands,
        results,
        scratch,
        scores * 40 * HD,
        scores,
    )


def partner(value, axis, mask):
    pairs = [(source, source ^ mask) for source in range(lax.axis_size(axis))]
    return lax.ppermute(value, axis, pairs)


def over_core(value):
    return partner(value, "cam", 1)


def over_x(value):
    return partner(value, "cam", 2)


def over_y(value):
    return partner(value, "dp", 1)


def over_z(value, apart_by):
    return partner(value, "dp", 2 * apart_by)


def stages_of(order):
    return (over_x, over_y) if order == "xy" else (over_y, over_x)


def by_blocks():
    return lax.axis_size("dp") * lax.axis_size("cam") == BLOCKS


def gather(shard, order):
    outer, inner = stages_of(order)
    if by_blocks():
        held = jnp.stack([shard] + [over_z(shard, n) for n in range(1, 4)])
        held = jnp.concatenate([held, inner(held)])
        held = jnp.concatenate([held, outer(held)])
        return held, over_core(held)
    full = lax.all_gather(shard, ("dp", "cam"), axis=shard.ndim - 2, tiled=True)
    full = full.reshape(*full.shape[:-2], 4, 2, 2, 2, ROWS, full.shape[-1])
    at = shard.ndim - 2
    x_at, y_at = at + 2, at + 1
    front = (at + 3, x_at, y_at, at) if order == "xy" else (at + 3, y_at, x_at, at)
    full = jnp.moveaxis(full, front, (0, 1, 2, 3))
    full = full.reshape(2, HALF, *full.shape[4:])
    return full[0], full[1]


def scatter(sides, order):
    outer, inner = stages_of(order)
    keep, send = sides
    if by_blocks():
        held = keep.astype(F32) + over_core(send).astype(F32)
        for stage in (outer, inner):
            half = held.shape[0] // 2
            held = held[:half] + stage(held[half:].astype(BF16)).astype(F32)
        sends = [over_z(held[n].astype(BF16), n).astype(F32) for n in range(1, 4)]
        return (held[0] + sends[0]) + (sends[1] + sends[2])
    full = jnp.stack([keep, send]).reshape(2, 2, 2, 4, ROWS, keep.shape[-1])
    places = (3, 2, 1, 0) if order == "xy" else (3, 1, 2, 0)
    full = jnp.moveaxis(full, (0, 1, 2, 3), places).reshape(D, keep.shape[-1])
    return lax.psum_scatter(full.astype(F32), ("dp", "cam"), scatter_dimension=0, tiled=True)


def total_of(vector):
    if by_blocks():
        for stage in (over_core, over_x, over_y):
            vector = vector + stage(vector)
        others = [over_z(vector, n) for n in range(1, 4)]
        return (vector + others[0]) + (others[1] + others[2])
    return lax.psum(vector, ("dp", "cam"))


def local(
    tokens,
    out_grad,
    joint_state,
    joint_mask,
    attn_master,
    attn_first,
    attn_second,
    attn_average,
    ffn_master,
    ffn_first,
    ffn_second,
    ffn_average,
    small_params,
    small_first,
    small_second,
    small_average,
):
    cam_index = lax.axis_index("cam")
    slot, group_index = cam_index % 4, cam_index // 4
    items_here, _, seg_len, _ = tokens.shape
    assert items_here == 4
    device = lax.axis_index("dp") * lax.axis_size("cam") + cam_index if by_blocks() else 0
    where = jnp.stack([jnp.int32(device), jnp.int32(slot)])

    def piece_for(array, n):
        return lax.dynamic_index_in_dim(array, slot ^ n, 0, keepdims=False)

    def trade(pieces):
        return [pieces[0]] + [partner(pieces[n], "cam", n) for n in range(1, 4)]

    def arrange(pieces):
        full = jnp.stack(pieces)
        return jnp.stack([lax.dynamic_index_in_dim(full, slot ^ n, 0, keepdims=False) for n in range(4)])

    sequence = trade([piece_for(tokens[:, 0], n) for n in range(4)])
    attn_low = attn_master.astype(BF16)
    ffn_low = ffn_master.astype(BF16)
    query_key = gather(attn_low[:2], "xy")
    value_out = gather(attn_low[2:], "yx")
    sides = (*query_key, *value_out)
    up = gather(ffn_low[0], "xy")
    down = gather(ffn_low[1], "yx")
    cotangents = trade([piece_for(out_grad[:, 0], n) for n in range(4)])

    vectors = small_params[: 8 * D].reshape(8, D)
    joint_rows = small_params[8 * D : (8 + NJ) * D].reshape(NJ, D)
    hidden_bias = small_params[(8 + NJ) * D :].reshape(1, -1)
    active = (joint_state * joint_mask.astype(F32))[slot, group_index]
    joint = jnp.sum(active[:, None] * joint_rows, axis=0, keepdims=True)

    rounded, top_rows, *heads = attend(0, where, [*sequence, joint], sides, vectors, seg_len)
    heads = [heads]
    for group in range(1, GROUPS):
        heads.append(attend(group, where, [rounded], sides, vectors, seg_len))
    mixed = [x[3] for x in heads]
    h1, y1, gated, slope, *rest = feed_forward(
        where, rounded, top_rows, mixed, value_out, up, down, vectors, hidden_bias, cotangents
    )
    out_pieces, dh2, grads_two = rest[:4], rest[4], rest[5]
    *weight_grads, hidden_grad, dh1, da, grads_one = feed_back(
        where, dh2, h1, y1, gated, slope, mixed, value_out, up, down, vectors
    )
    block_output = arrange(trade(out_pieces)).reshape(tokens.shape)
    up_grad = scatter(weight_grads[0:2], "xy")
    down_grad = scatter(weight_grads[2:4], "yx")
    out_proj_grad = scatter(weight_grads[4:6], "yx")

    before, pair_grads, bias_grads = dh1, [], []
    for group in range(GROUPS):
        results = attend_back(
            group, where, heads[group][:4], da, heads[group][4], rounded, before, sides, seg_len
        )
        pair_sides, rest = results[: 2 * GROUP_PAIRS], results[2 * GROUP_PAIRS :]
        bias_grad, before, rest = rest[0], rest[1], rest[2:]
        bias_grads.append(bias_grad)
        for n in range(GROUP_PAIRS):
            pair_grads.append(scatter(pair_sides[2 * n : 2 * n + 2], pair_order(n)))
    *sends, item_top = rest
    grad_pieces = [x.astype(F32) for x in trade([before, *sends])[1:]]
    input_grad = arrange([before, *grad_pieces]).reshape(tokens.shape)

    bias_grads = jnp.concatenate(bias_grads, axis=1)
    small_grad = jnp.concatenate(
        [
            bias_grads[0],
            bias_grads[1],
            grads_one[2],
            grads_one[0],
            grads_one[1],
            grads_two[2],
            grads_two[0],
            grads_two[1],
            (active[:, None] * item_top[1:2]).reshape(-1),
            hidden_grad[0],
        ]
    )
    small_total = total_of(small_grad)
    rows_here = attn_master.shape[1]
    proj_grad = jnp.stack(pair_grads, axis=1).reshape(rows_here, PAIRS, 3, PAIR)
    proj_grad = jnp.moveaxis(proj_grad, 2, 0).reshape(3, rows_here, D)
    attn_shard = jnp.concatenate([proj_grad, out_proj_grad[None]])
    ffn_shard = jnp.stack([up_grad, down_grad])
    new_attn = adam_update(
        attn_master, attn_shard, attn_first, attn_second, attn_average, rate_matrix, decay_matrix
    )
    new_ffn = adam_update(
        ffn_master, ffn_shard, ffn_first, ffn_second, ffn_average, rate_matrix, decay_matrix
    )
    new_small = adam_update(
        small_params, small_total, small_first, small_second, small_average, rate_small, 0.0
    )
    return (block_output, input_grad, *new_attn, *new_ffn, *new_small)


def solution(mesh):
    in_specs = (
        P("dp", "cam", None, None),
        P("dp", "cam", None, None),
        P("dp", None, None),
        P("dp", None, None),
        P(None, ("dp", "cam"), None),
        P(None, ("dp", "cam"), None),
        P(None, ("dp", "cam"), None),
        P(None, ("dp", "cam"), None),
        P(None, ("dp", "cam"), None),
        P(None, ("dp", "cam"), None),
        P(None, ("dp", "cam"), None),
        P(None, ("dp", "cam"), None),
        P(),
        P(),
        P(),
        P(),
    )
    out_specs = (
        P("dp", "cam", None, None),
        P("dp", "cam", None, None),
        P(None, ("dp", "cam"), None),
        P(None, ("dp", "cam"), None),
        P(None, ("dp", "cam"), None),
        P(None, ("dp", "cam"), None),
        P(None, ("dp", "cam"), None),
        P(None, ("dp", "cam"), None),
        P(None, ("dp", "cam"), None),
        P(None, ("dp", "cam"), None),
        P(),
        P(),
        P(),
        P(),
    )
    return jax.shard_map(local, mesh=mesh, in_specs=in_specs, out_specs=out_specs, check_vma=False)
```

time: 697 us -> 408 us (0.59)
  matrix products: 237 us -> 0 us
  Pallas kernels: 0 us -> 145 us
  waiting for transfers between devices: 260 us -> 116 us
  starting transfers between devices: 6.73 us -> 89.8 us
  other arithmetic: 69.3 us -> 19.6 us
  blocking collectives: 39.5 us -> 0 us
  local copies, waits for them, and re-layouts: 57.7 us -> 31.8 us
  between operations: 15.1 us -> 1.92 us
    dot_general x69 -> x0, matrix products: 237 us -> none  [the longest x1 42.4 us: local(): jnp.dot(normed_low, ffn_full[0], preferred_element_type=jnp.float32)]
    reduce_scatter x1 -> x0, waiting for transfers between devices: 157 us -> none  [local(): lax.psum_scatter(ffn_grad, ('dp', 'cam'), scatter_dimension=1, tiled=True)]
    pallas_call x0 -> x6, Pallas kernels: none -> 145 us  [call(): pl.pallas_call(kernel, grid_spec=pltpu.PrefetchScalarGridSpec(num_scalar_...]
    ppermute x6 -> x84, starting transfers between devices: 6.56 us -> 89.8 us  [partner(): return lax.ppermute(value, axis, pairs)]
    ppermute x6 -> x84, waiting for transfers between devices: 57.2 us -> 116 us  [partner(): return lax.ppermute(value, axis, pairs)]
    psum x1 -> x0, blocking collectives: 39.5 us -> none  [local(): small_total = lax.psum(small_grad, ('dp', 'cam'))]
    unnamed x5 -> x0, waiting for transfers between devices: 32.3 us -> none
    another operation x13 -> x19, other arithmetic: 20.5 us -> 3.17 us  [the longest x1 10.4 us: local(): ffn_grad = jnp.stack([up_grad, down_grad])]
  transfers between devices with their start and end apart: 10 -> 84, of which waited for: 7 -> 31; matrix products, arithmetic and copies ran while one was open for 19% -> 11% of each run, Pallas kernels for 0% -> 7%
where the time goes in v1:
time: 408 us; the launch traced here: 403 us
  Pallas kernels  145 us (36%)
  waiting for transfers between devices  116 us (28%)
  starting transfers between devices  89.8 us (22%)
  local copies, waits for them, and re-layouts  31.8 us (8%)
  other arithmetic  19.6 us (5%)
    pallas_call x6, Pallas kernels, call(): pl.pallas_call(kernel, grid_spec=pltpu.PrefetchScalarGridSpec(num_scalar_...  145 us
    ppermute x84, waiting for transfers between devices, partner(): return lax.ppermute(value, axis, pairs)  116 us
    ppermute x84, starting transfers between devices, partner(): return lax.ppermute(value, axis, pairs)  89.8 us
    unnamed x102, local copies, waits for them, and re-layouts  11.3 us
  transfers between devices with their start and end apart: 84, of which 31 were waited for; matrix products, arithmetic and copies ran while one was open for 11% of the time, Pallas kernels for 7%

profile of v1, /device:TPU:0, one launch (start us, length us, event | category | flops | bytes accessed | tf_op | source)
XLA Modules:
  0.0 403.3 jit_solution(15087928586824966902)
XLA Ops:
  2.6 3.0 collective-permute-start.21
  5.6 2.6 collective-permute-start.22
  9.2 3.5 collective-permute-start.10
  14.1 2.2 collective-permute-start.11
  17.0 2.6 collective-permute-done.10
  20.2 3.3 collective-permute-start.4
  24.2 2.1 collective-permute-start.5
  27.9 2.4 collective-permute-done.5
  30.9 2.2 collective-permute-start.17
  33.1 1.6 collective-permute-start.12
  34.8 1.6 collective-permute-start.6
  37.7 1.6 collective-permute-start.18
  46.4 2.3 collective-permute-done.24
  51.7 1.5 collective-permute-start.19
  53.9 1.9 collective-permute-done.13
  58.6 13.8 %collective-permute-done.25 = bf16[8,16,3200]{2,1,0:T(8,128)(2,1)S(1)} collective-permute-done((bf16[8,16,3200]{2,1,0:T(8,128)(2,1)S(1)}, bf16[8,16,3200]{2,1,0:T(8,128)(2,1)S(1)}, u32[]{:S(2)}, u32[]{:S(2)}) %collective-permute-start.25) | collective-permute-done | bytes 819232 | tf_op jit(solution)/shard_map/ppermute | solution.py:525
  79.4 7.7 %collective-permute-done.2.refs_3_ = bf16[304,512]{1,0:T(8,128)(2,1)S(1)} collective-permute-done((bf16[304,512]{1,0:T(8,128)(2,1)S(1)}, bf16[304,512]{1,0:T(8,128)(2,1)S(1)}, u32[]{:S(2)}, u32[]{:S(2)}) %collective-permute-start.2) | collective-permute-done | bytes 311328 | tf_op jit(solution)/shard_map/ppermute | solution.py:525
  89.0 14.7 %attend_0.1 = (bf16[1216,512]{1,0:T(8,128)(2,1)}, f32[8,512]{1,0:T(8,128)}, bf16[1216,256]{1,0:T(8,128)(2,1)}, bf16[1216,256]{1,0:T(8,128)(2,1)}, bf16[1216,256]...) custom-call(s32[2]{0:T(128)} %pad_add_fusion.where, bf16[304,512]{1,0:T(8,128)(2,1)} %get-tuple-element.206.refs_0_, ...), custom_call_target="tpu_custom_call" | custom-call | flops 6056574976 | bytes 7119872 | tf_op jit(solution)/shard_map/attend_0/pallas_call | solution.py:376
  103.6 13.8 %attend_1.1 = (bf16[1216,256]{1,0:T(8,128)(2,1)}, bf16[1216,256]{1,0:T(8,128)(2,1)}, bf16[1216,256]{1,0:T(8,128)(2,1)}, bf16[1216,256]{1,0:T(8,128)(2,1)}, f32[2,2,1216]{2,1,0:T(2,128)}) custom-call(s32[2]{0:T(128)} %pad_add_fusion.where, bf16[1216,512]{1,0:T(8,128)(2,1)} %get-tuple-element.62.refs_0_.refs_6_, ...), custom_call_target="tpu_custom_call" | custom-call | flops 6056574976 | bytes 5856256 | tf_op jit(solution)/shard_map/attend_1/pallas_call | solution.py:376
  118.3 31.7 %feed_forward.1 = (f32[1216,512]{1,0:T(8,128)}, bf16[1216,512]{1,0:T(8,128)(2,1)}, bf16[1216,3200]{1,0:T(8,128)(2,1)}, bf16[1216,3200]{1,0:T(8,128)(2,1)}, bf16[...) custom-call(s32[2]{0:T(128)} %pad_add_fusion.where, ...), custom_call_target="tpu_custom_call" | custom-call | flops 8606711808 | bytes 34435584 | tf_op jit(solution)/shard_map/feed_forward/pallas_call | solution.py:376
  150.0 35.0 %feed_back.1 = (bf16[16,16,3200]{2,1,0:T(8,128)(2,1)}, bf16[16,16,3200]{2,1,0:T(8,128)(2,1)}, bf16[16,16,3200]{2,1,0:T(8,128)(2,1)}, bf16[16,16,3200]{2,1,0:T(8,...) custom-call(s32[2]{0:T(128)} %pad_add_fusion.where, ...), custom_call_target="tpu_custom_call" | custom-call | flops 17213423616 | bytes 41497088 | tf_op jit(solution)/shard_map/feed_back/pallas_call | solution.py:376
  185.0 24.5 %attend_back_0.1 = (bf16[16,16,384]{2,1,0:T(8,128)(2,1)}, bf16[16,16,384]{2,1,0:T(8,128)(2,1)}, bf16[16,16,384]{2,1,0:T(8,128)(2,1)}, bf16[16,16,384]{2,1,0:T(8,...) custom-call(s32[2]{0:T(128)} %pad_add_fusion.where, bf16[1216,256]{1,0:T(8,128)(2,1)} %get-tuple-element.80.refs_0_, ...), custom_call_target="tpu_custom_call" | custom-call | flops 15141437440 | bytes 12872704 | tf_op jit(solution)/shard_map/attend_back_0/pallas_call | solution.py:376
  210.3 24.9 %attend_back_1.1 = (bf16[16,16,384]{2,1,0:T(8,128)(2,1)}, bf16[16,16,384]{2,1,0:T(8,128)(2,1)}, bf16[16,16,384]{2,1,0:T(8,128)(2,1)}, bf16[16,16,384]{2,1,0:T(8,...) custom-call(s32[2]{0:T(128)} %pad_add_fusion.where, ...), custom_call_target="tpu_custom_call" | custom-call | flops 15141437440 | bytes 11955200 | tf_op jit(solution)/shard_map/attend_back_1/pallas_call | solution.py:376
  241.8 2.9 collective-permute-done.79
  244.7 1.6 collective-permute-start.80
  246.8 2.2 collective-permute-done.80
  249.7 3.0 collective-permute-done.42
  255.2 2.2 collective-permute-start.83
  257.6 4.5 %collective-permute-done.82 = f32[14464]{0:T(1024)S(1)} collective-permute-done((f32[14464]{0:T(1024)S(1)}, f32[14464]{0:T(1024)S(1)}, u32[]{:S(2)}, u32[]{:S(2)}) %collective-permute-start.82) | collective-permute-done | bytes 57888 | tf_op jit(solution)/shard_map/ppermute | solution.py:525
  265.0 15.0 %collective-permute-done.37 = bf16[8,16,384]{2,1,0:T(8,128)(2,1)S(1)} collective-permute-done((bf16[8,16,384]{2,1,0:T(8,128)(2,1)S(1)}, bf16[8,16,384]{2,1,0:T(8,128)(2,1)S(1)}, u32[]{:S(2)}, u32[]{:S(2)}) %collective-permute-start.37) | collective-permute-done | bytes 98336 | tf_op jit(solution)/shard_map/ppermute | solution.py:525
  280.7 4.2 %collective-permute-done.43 = bf16[8,16,384]{2,1,0:T(8,128)(2,1)S(1)} collective-permute-done((bf16[8,16,384]{2,1,0:T(8,128)(2,1)S(1)}, bf16[8,16,384]{2,1,0:T(8,128)(2,1)S(1)}, u32[]{:S(2)}, u32[]{:S(2)}) %collective-permute-start.43) | collective-permute-done | bytes 98336 | tf_op jit(solution)/shard_map/ppermute | solution.py:525
  285.6 3.9 collective-permute-done.49
  290.1 4.0 collective-permute-done.55
  297.7 7.4 %collective-permute-done.31 = bf16[304,512]{1,0:T(8,128)(2,1)S(1)} collective-permute-done((bf16[304,512]{1,0:T(8,128)(2,1)S(1)}, bf16[304,512]{1,0:T(8,128)(2,1)S(1)}, u32[]{:S(2)}, u32[]{:S(2)}) %collective-permute-start.31) | collective-permute-done | bytes 311328 | tf_op jit(solution)/shard_map/ppermute | solution.py:525
  305.9 4.1 %collective-permute-done.32 = bf16[304,512]{1,0:T(8,128)(2,1)S(1)} collective-permute-done((bf16[304,512]{1,0:T(8,128)(2,1)S(1)}, bf16[304,512]{1,0:T(8,128)(2,1)S(1)}, u32[]{:S(2)}, u32[]{:S(2)}) %collective-permute-start.32) | collective-permute-done | bytes 311328 | tf_op jit(solution)/shard_map/ppermute | solution.py:525
  310.8 1.7 maximum_bitcast_fusion
  314.9 2.5 collective-permute-start.40
  318.3 1.9 collective-permute-start.41
  320.3 2.4 collective-permute-start.46
  323.8 1.9 collective-permute-start.47
  326.3 2.5 collective-permute-start.52
  329.2 1.9 collective-permute-start.53
  331.8 1.6 collective-permute-start.61
  336.8 1.9 collective-permute-start.59
  340.1 2.1 collective-permute-done.59
  342.9 1.4 stack.176
  344.2 1.4 stack.177
  348.3 1.5 fusion.32
  350.5 2.5 collective-permute-start.64
  352.9 1.9 collective-permute-start.65
  355.8 2.6 collective-permute-done.65
  359.2 2.0 multiply_add_fusion.3
  361.2 1.8 convert_add_fusion.1
  364.8 1.5 collective-permute-start.73
  366.3 13.2 %collective-permute-done.67 = bf16[8,16,3200]{2,1,0:T(8,128)(2,1)S(1)} collective-permute-done((bf16[8,16,3200]{2,1,0:T(8,128)(2,1)S(1)}, bf16[8,16,3200]{2,1,0:T(8,128)(2,1)S(1)}, u32[]{:S(2)}, u32[]{:S(2)}) %collective-permute-start.67) | collective-permute-done | bytes 819232 | tf_op jit(solution)/shard_map/ppermute | solution.py:525
  379.7 1.5 collective-permute-start.68
  381.2 1.8 collective-permute-done.73
  383.8 4.0 collective-permute-done.68
  387.9 2.5 collective-permute-start.70
  390.4 1.9 collective-permute-start.71
  392.6 2.5 collective-permute-start.76
  395.1 1.9 collective-permute-start.77
  398.4 3.3 collective-permute-done.76
  401.7 1.4 multiply_add_fusion.1
  (323 shorter events, 75.4 us)
Async XLA Ops:
  2.6 28.3 %collective-permute-start.21 = (bf16[16,3200]{1,0:T(8,128)(2,1)S(1)}, bf16[16,3200]{1,0:T(8,128)(2,1)S(1)}, u32[]{:S(2)}, u32[]{:S(2)}) collective-permute-start(bf16[16,3200]{1,0:T(8,128)(2,1)S(1)} %get-tuple-element.222), channel_id=1, source_target_pairs={{0,8},{4,12},{8,0},{12,4},{16,24},{20,28},{24,16},{28,20},{1,9},{5... | collective-permute-start | bytes 307208 | tf_op jit(solution)/shard_map/ppermute | solution.py:525
  5.6 27.5 %collective-permute-start.22 = (bf16[16,3200]{1,0:T(8,128)(2,1)S(1)}, bf16[16,3200]{1,0:T(8,128)(2,1)S(1)}, u32[]{:S(2)}, u32[]{:S(2)}) collective-permute-start(bf16[16,3200]{1,0:T(8,128)(2,1)S(1)} %get-tuple-element.222), channel_id=1, source_target_pairs={{0,16},{4,20},{8,24},{12,28},{16,0},{20,4},{24,8},{28,12},{1,17},{... | collective-permute-start | bytes 307208 | tf_op jit(solution)/shard_map/ppermute | solution.py:525
  8.2 24.9 %collective-permute-start.23 = (bf16[16,3200]{1,0:T(8,128)(2,1)S(1)}, bf16[16,3200]{1,0:T(8,128)(2,1)S(1)}, u32[]{:S(2)}, u32[]{:S(2)}) collective-permute-start(bf16[16,3200]{1,0:T(8,128)(2,1)S(1)} %get-tuple-element.222), channel_id=1, source_target_pairs={{0,24},{4,28},{8,16},{12,20},{16,8},{20,12},{24,0},{28,4},{1,25},{... | collective-permute-start | bytes 307208 | tf_op jit(solution)/shard_map/ppermute | solution.py:525
  8.2 5.9 %collective-permute-start.9 = (bf16[2,16,512]{2,1,0:T(8,128)(2,1)S(1)}, bf16[2,16,512]{2,1,0:T(8,128)(2,1)S(1)}, u32[]{:S(2)}, u32[]{:S(2)}) collective-permute-start(bf16[2,16,512]{2,1,0:T(8,128)(2,1)S(1)} %get-tuple-element.251), channel_id=1, source_target_pairs={{0,8},{4,12},{8,0},{12,4},{16,24},{20,28},{24,16},{28,20},{1,9},{5... | collective-permute-start | bytes 98312 | tf_op jit(solution)/shard_map/ppermute | solution.py:525
  9.2 10.3 %collective-permute-start.10 = (bf16[2,16,512]{2,1,0:T(8,128)(2,1)S(1)}, bf16[2,16,512]{2,1,0:T(8,128)(2,1)S(1)}, u32[]{:S(2)}, u32[]{:S(2)}) collective-permute-start(bf16[2,16,512]{2,1,0:T(8,128)(2,1)S(1)} %get-tuple-element.251), channel_id=1, source_target_pairs={{0,16},{4,20},{8,24},{12,28},{16,0},{20,4},{24,8},{28,12},{1,17},{... | collective-permute-start | bytes 98312 | tf_op jit(solution)/shard_map/ppermute | solution.py:525
  14.1 6.1 %collective-permute-start.11 = (bf16[2,16,512]{2,1,0:T(8,128)(2,1)S(1)}, bf16[2,16,512]{2,1,0:T(8,128)(2,1)S(1)}, u32[]{:S(2)}, u32[]{:S(2)}) collective-permute-start(bf16[2,16,512]{2,1,0:T(8,128)(2,1)S(1)} %get-tuple-element.251), channel_id=1, source_target_pairs={{0,24},{4,28},{8,16},{12,20},{16,8},{20,12},{24,0},{28,4},{1,25},{... | collective-permute-start | bytes 98312 | tf_op jit(solution)/shard_map/ppermute | solution.py:525
  20.2 6.7 %collective-permute-start.4 = (bf16[2,16,512]{2,1,0:T(8,128)(2,1)S(1)}, bf16[2,16,512]{2,1,0:T(8,128)(2,1)S(1)}, u32[]{:S(2)}, u32[]{:S(2)}) collective-permute-start(bf16[2,16,512]{2,1,0:T(8,128)(2,1)S(1)} %get-tuple-element.252), channel_id=1, source_target_pairs={{0,16},{4,20},{8,24},{12,28},{16,0},{20,4},{24,8},{28,12},{1,17},{... | collective-permute-start | bytes 98312 | tf_op jit(solution)/shard_map/ppermute | solution.py:525
  24.2 6.1 %collective-permute-start.5 = (bf16[2,16,512]{2,1,0:T(8,128)(2,1)S(1)}, bf16[2,16,512]{2,1,0:T(8,128)(2,1)S(1)}, u32[]{:S(2)}, u32[]{:S(2)}) collective-permute-start(bf16[2,16,512]{2,1,0:T(8,128)(2,1)S(1)} %get-tuple-element.252), channel_id=1, source_target_pairs={{0,24},{4,28},{8,16},{12,20},{16,8},{20,12},{24,0},{28,4},{1,25},{... | collective-permute-start | bytes 98312 | tf_op jit(solution)/shard_map/ppermute | solution.py:525
  26.9 7.9 %collective-permute-start.15 = (bf16[16,3200]{1,0:T(8,128)(2,1)S(1)}, bf16[16,3200]{1,0:T(8,128)(2,1)S(1)}, u32[]{:S(2)}, u32[]{:S(2)}) collective-permute-start(bf16[16,3200]{1,0:T(8,128)(2,1)S(1)} %get-tuple-element.219), channel_id=1, source_target_pairs={{0,8},{4,12},{8,0},{12,4},{16,24},{20,28},{24,16},{28,20},{1,9},{5... | collective-permute-start | bytes 307208 | tf_op jit(solution)/shard_map/ppermute | solution.py:525
  30.2 6.1 %collective-permute-start.16 = (bf16[16,3200]{1,0:T(8,128)(2,1)S(1)}, bf16[16,3200]{1,0:T(8,128)(2,1)S(1)}, u32[]{:S(2)}, u32[]{:S(2)}) collective-permute-start(bf16[16,3200]{1,0:T(8,128)(2,1)S(1)} %get-tuple-element.219), channel_id=1, source_target_pairs={{0,16},{4,20},{8,24},{12,28},{16,0},{20,4},{24,8},{28,12},{1,17},{... | collective-permute-start | bytes 307208 | tf_op jit(solution)/shard_map/ppermute | solution.py:525
  30.9 6.7 %collective-permute-start.17 = (bf16[16,3200]{1,0:T(8,128)(2,1)S(1)}, bf16[16,3200]{1,0:T(8,128)(2,1)S(1)}, u32[]{:S(2)}, u32[]{:S(2)}) collective-permute-start(bf16[16,3200]{1,0:T(8,128)(2,1)S(1)} %get-tuple-element.219), channel_id=1, source_target_pairs={{0,24},{4,28},{8,16},{12,20},{16,8},{20,12},{24,0},{28,4},{1,25},{... | collective-permute-start | bytes 307208 | tf_op jit(solution)/shard_map/ppermute | solution.py:525
  33.1 41.7 %collective-permute-start = (bf16[304,512]{1,0:T(8,128)(2,1)S(1)}, bf16[304,512]{1,0:T(8,128)(2,1)S(1)}, u32[]{:S(2)}, u32[]{:S(2)}) collective-permute-start(bf16[304,512]{1,0:T(8,128)(2,1)S(1)} %get-tuple-element.205), channel_id=1, source_target_pairs={{0,1},{1,0},{2,3},{3,2},{4,5},{5,4},{6,7},{7,6},{8,9},{9,8},{10,11... | collective-permute-start | bytes 933896 | tf_op jit(solution)/shard_map/ppermute | solution.py:525
  33.1 10.1 %collective-permute-start.12 = (bf16[4,2,16,512]{3,2,1,0:T(8,128)(2,1)S(1)}, bf16[4,2,16,512]{3,2,1,0:T(8,128)(2,1)S(1)}, u32[]{:S(2)}, u32[]{:S(2)}) collective-permute-start(bf16[4,2,16,512]{3,2,1,0:T(8,128)(2,1)S(1)} %pad_maximum_fusion.6), channel_id=1, source_target_pairs={{0,2},{1,3},{2,0},{3,1},{4,6},{5,7},{6,4},{7,5},{8,10},{9,11},{10,... | collective-permute-start | bytes 393224 | tf_op jit(solution)/shard_map/ppermute | solution.py:525
  34.8 9.7 %collective-permute-start.6 = (bf16[4,2,16,512]{3,2,1,0:T(8,128)(2,1)S(1)}, bf16[4,2,16,512]{3,2,1,0:T(8,128)(2,1)S(1)}, u32[]{:S(2)}, u32[]{:S(2)}) collective-permute-start(bf16[4,2,16,512]{3,2,1,0:T(8,128)(2,1)S(1)} %pad_maximum_fusion.5), channel_id=1, source_target_pairs={{0,4},{4,0},{8,12},{12,8},{16,20},{20,16},{24,28},{28,24},{1,5},{5... | collective-permute-start | bytes 393224 | tf_op jit(solution)/shard_map/ppermute | solution.py:525
  36.4 12.3 %collective-permute-start.24 = (bf16[4,16,3200]{2,1,0:T(8,128)(2,1)S(1)}, bf16[4,16,3200]{2,1,0:T(8,128)(2,1)S(1)}, u32[]{:S(2)}, u32[]{:S(2)}) collective-permute-start(bf16[4,16,3200]{2,1,0:T(8,128)(2,1)S(1)} %pad_maximum_fusion.3), channel_id=1, source_target_pairs={{0,2},{1,3},{2,0},{3,1},{4,6},{5,7},{6,4},{7,5},{8,10},{9,11},{10,... | collective-permute-start | bytes 1228808 | tf_op jit(solution)/shard_map/ppermute | solution.py:525
  37.7 13.2 %collective-permute-start.18 = (bf16[4,16,3200]{2,1,0:T(8,128)(2,1)S(1)}, bf16[4,16,3200]{2,1,0:T(8,128)(2,1)S(1)}, u32[]{:S(2)}, u32[]{:S(2)}) collective-permute-start(bf16[4,16,3200]{2,1,0:T(8,128)(2,1)S(1)} %pad_maximum_fusion.2), channel_id=1, source_target_pairs={{0,4},{4,0},{8,12},{12,8},{16,20},{20,16},{24,28},{28,24},{1,5},{5... | collective-permute-start | bytes 1228808 | tf_op jit(solution)/shard_map/ppermute | solution.py:525
  43.9 11.9 %collective-permute-start.13 = (bf16[8,2,16,512]{3,2,1,0:T(8,128)(2,1)S(1)}, bf16[8,2,16,512]{3,2,1,0:T(8,128)(2,1)S(1)}, u32[]{:S(2)}, u32[]{:S(2)}) collective-permute-start(bf16[8,2,16,512]{3,2,1,0:T(8,128)(2,1)S(1)} %get-tuple-element.226), channel_id=1, source_target_pairs={{0,4},{4,0},{8,12},{12,8},{16,20},{20,16},{24,28},{28,24},{1,5},{5... | collective-permute-start | bytes 786440 | tf_op jit(solution)/shard_map/ppermute | solution.py:525
  45.1 12.8 %collective-permute-start.7 = (bf16[8,2,16,512]{3,2,1,0:T(8,128)(2,1)S(1)}, bf16[8,2,16,512]{3,2,1,0:T(8,128)(2,1)S(1)}, u32[]{:S(2)}, u32[]{:S(2)}) collective-permute-start(bf16[8,2,16,512]{3,2,1,0:T(8,128)(2,1)S(1)} %get-tuple-element.228), channel_id=1, source_target_pairs={{0,2},{1,3},{2,0},{3,1},{4,6},{5,7},{6,4},{7,5},{8,10},{9,11},{10,... | collective-permute-start | bytes 786440 | tf_op jit(solution)/shard_map/ppermute | solution.py:525
  49.5 22.8 %collective-permute-start.25 = (bf16[8,16,3200]{2,1,0:T(8,128)(2,1)S(1)}, bf16[8,16,3200]{2,1,0:T(8,128)(2,1)S(1)}, u32[]{:S(2)}, u32[]{:S(2)}) collective-permute-start(bf16[8,16,3200]{2,1,0:T(8,128)(2,1)S(1)} %get-tuple-element.214), channel_id=1, source_target_pairs={{0,4},{4,0},{8,12},{12,8},{16,20},{20,16},{24,28},{28,24},{1,5},{5... | collective-permute-start | bytes 2457608 | tf_op jit(solution)/shard_map/ppermute | solution.py:525
  51.7 21.6 %collective-permute-start.19 = (bf16[8,16,3200]{2,1,0:T(8,128)(2,1)S(1)}, bf16[8,16,3200]{2,1,0:T(8,128)(2,1)S(1)}, u32[]{:S(2)}, u32[]{:S(2)}) collective-permute-start(bf16[8,16,3200]{2,1,0:T(8,128)(2,1)S(1)} %get-tuple-element.216), channel_id=1, source_target_pairs={{0,2},{1,3},{2,0},{3,1},{4,6},{5,7},{6,4},{7,5},{8,10},{9,11},{10,... | collective-permute-start | bytes 2457608 | tf_op jit(solution)/shard_map/ppermute | solution.py:525
  55.8 22.0 %collective-permute-start.1 = (bf16[304,512]{1,0:T(8,128)(2,1)S(1)}, bf16[304,512]{1,0:T(8,128)(2,1)}, u32[]{:S(2)}, u32[]{:S(2)}) collective-permute-start(bf16[304,512]{1,0:T(8,128)(2,1)S(1)} %get-tuple-element.207), channel_id=1, source_target_pairs={{0,2},{1,3},{2,0},{3,1},{4,6},{5,7},{6,4},{7,5},{8,10},{9,11},{10,... | collective-permute-start | bytes 933896 | tf_op jit(solution)/shard_map/ppermute | solution.py:525
  57.9 29.4 %collective-permute-start.14 = (bf16[16,2,16,512]{3,2,1,0:T(8,128)(2,1)}, bf16[16,2,16,512]{3,2,1,0:T(8,128)(2,1)S(1)}, u32[]{:S(2)}, u32[]{:S(2)}) collective-permute-start(bf16[16,2,16,512]{3,2,1,0:T(8,128)(2,1)} %constant_dynamic-update-slice_fusion.16.refs_7_.refs_3_.refs_4_.refs_10_), channel_id=1, source_target_pairs={{0,1},{1,0},{2,3},{3,2},{4,5},{5,4},{6,7},{7,6},{8,9},{9,8},{10,11... | collective-permute-start | bytes 1572872 | tf_op jit(solution)/shard_map/ppermute | solution.py:525
  72.3 16.2 %collective-permute-start.8 = (bf16[16,2,16,512]{3,2,1,0:T(8,128)(2,1)}, bf16[16,2,16,512]{3,2,1,0:T(8,128)(2,1)}, u32[]{:S(2)}, u32[]{:S(2)}) collective-permute-start(bf16[16,2,16,512]{3,2,1,0:T(8,128)(2,1)} %constant_dynamic-update-slice_fusion.5.refs_5_.refs_1_.refs_8_), channel_id=1, source_target_pairs={{0,1},{1,0},{2,3},{3,2},{4,5},{5,4},{6,7},{7,6},{8,9},{9,8},{10,11... | collective-permute-start | bytes 1572872 | tf_op jit(solution)/shard_map/ppermute | solution.py:525
  73.3 44.2 %collective-permute-start.26 = (bf16[16,16,3200]{2,1,0:T(8,128)(2,1)}, bf16[16,16,3200]{2,1,0:T(8,128)(2,1)}, u32[]{:S(2)}, u32[]{:S(2)}) collective-permute-start(bf16[16,16,3200]{2,1,0:T(8,128)(2,1)} %constant_dynamic-update-slice_fusion.38.refs_8_.refs_11_), channel_id=1, source_target_pairs={{0,1},{1,0},{2,3},{3,2},{4,5},{5,4},{6,7},{7,6},{8,9},{9,8},{10,11... | collective-permute-start | bytes 4915208 | tf_op jit(solution)/shard_map/ppermute | solution.py:525
  74.8 42.7 %collective-permute-start.20 = (bf16[16,16,3200]{2,1,0:T(8,128)(2,1)}, bf16[16,16,3200]{2,1,0:T(8,128)(2,1)}, u32[]{:S(2)}, u32[]{:S(2)}) collective-permute-start(bf16[16,16,3200]{2,1,0:T(8,128)(2,1)} %constant_dynamic-update-slice_fusion.27.refs_6_.refs_9_), channel_id=1, source_target_pairs={{0,1},{1,0},{2,3},{3,2},{4,5},{5,4},{6,7},{7,6},{8,9},{9,8},{10,11... | collective-permute-start | bytes 4915208 | tf_op jit(solution)/shard_map/ppermute | solution.py:525
  77.8 9.3 %collective-permute-start.2 = (bf16[304,512]{1,0:T(8,128)(2,1)S(1)}, bf16[304,512]{1,0:T(8,128)(2,1)S(1)}, u32[]{:S(2)}, u32[]{:S(2)}) collective-permute-start(bf16[304,512]{1,0:T(8,128)(2,1)S(1)} %get-tuple-element.204), channel_id=1, source_target_pairs={{0,3},{1,2},{2,1},{3,0},{4,7},{5,6},{6,5},{7,4},{8,11},{9,10},{10,... | collective-permute-start | bytes 933896 | tf_op jit(solution)/shard_map/ppermute | solution.py:525
  87.1 30.3 %collective-permute-start.27 = (bf16[304,512]{1,0:T(8,128)(2,1)S(1)}, bf16[304,512]{1,0:T(8,128)(2,1)S(1)}, u32[]{:S(2)}, u32[]{:S(2)}) collective-permute-start(bf16[304,512]{1,0:T(8,128)(2,1)S(1)} %get-tuple-element.201), channel_id=1, source_target_pairs={{0,1},{1,0},{2,3},{3,2},{4,5},{5,4},{6,7},{7,6},{8,9},{9,8},{10,11... | collective-permute-start | bytes 933896 | tf_op jit(solution)/shard_map/ppermute | solution.py:525
  87.3 30.2 %collective-permute-start.28 = (bf16[304,512]{1,0:T(8,128)(2,1)S(1)}, bf16[304,512]{1,0:T(8,128)(2,1)S(1)}, u32[]{:S(2)}, u32[]{:S(2)}) collective-permute-start(bf16[304,512]{1,0:T(8,128)(2,1)S(1)} %get-tuple-element.203), channel_id=1, source_target_pairs={{0,2},{1,3},{2,0},{3,1},{4,6},{5,7},{6,4},{7,5},{8,10},{9,11},{10,... | collective-permute-start | bytes 933896 | tf_op jit(solution)/shard_map/ppermute | solution.py:525
  88.5 28.9 %collective-permute-start.29 = (bf16[304,512]{1,0:T(8,128)(2,1)S(1)}, bf16[304,512]{1,0:T(8,128)(2,1)S(1)}, u32[]{:S(2)}, u32[]{:S(2)}) collective-permute-start(bf16[304,512]{1,0:T(8,128)(2,1)S(1)} %get-tuple-element.200), channel_id=1, source_target_pairs={{0,3},{1,2},{2,1},{3,0},{4,7},{5,6},{6,5},{7,4},{8,11},{9,10},{10,... | collective-permute-start | bytes 933896 | tf_op jit(solution)/shard_map/ppermute | solution.py:525
  238.4 10.6 %collective-permute-start.36 = (bf16[16,16,384]{2,1,0:T(8,128)(2,1)S(1)}, bf16[16,16,384]{2,1,0:T(8,128)(2,1)S(1)}, u32[]{:S(2)}, u32[]{:S(2)}) collective-permute-start(bf16[16,16,384]{2,1,0:T(8,128)(2,1)S(1)} %copy-done.38), channel_id=1, source_target_pairs={{0,1},{1,0},{2,3},{3,2},{4,5},{5,4},{6,7},{7,6},{8,9},{9,8},{10,11... | collective-permute-start | bytes 589832 | tf_op jit(solution)/shard_map/ppermute | solution.py:525
  246.3 114.9 %collective-permute-start.66 = (bf16[16,16,3200]{2,1,0:T(8,128)(2,1)}, bf16[16,16,3200]{2,1,0:T(8,128)(2,1)}, u32[]{:S(2)}, u32[]{:S(2)}) collective-permute-start(bf16[16,16,3200]{2,1,0:T(8,128)(2,1)} %get-tuple-element.101), channel_id=1, source_target_pairs={{0,1},{1,0},{2,3},{3,2},{4,5},{5,4},{6,7},{7,6},{8,9},{9,8},{10,11... | collective-permute-start | bytes 4915208 | tf_op jit(solution)/shard_map/ppermute | solution.py:525
  246.3 117.6 %collective-permute-start.72 = (bf16[16,16,3200]{2,1,0:T(8,128)(2,1)}, bf16[16,16,3200]{2,1,0:T(8,128)(2,1)S(1)}, u32[]{:S(2)}, u32[]{:S(2)}) collective-permute-start(bf16[16,16,3200]{2,1,0:T(8,128)(2,1)} %get-tuple-element.103), channel_id=1, source_target_pairs={{0,1},{1,0},{2,3},{3,2},{4,5},{5,4},{6,7},{7,6},{8,9},{9,8},{10,11... | collective-permute-start | bytes 4915208 | tf_op jit(solution)/shard_map/ppermute | solution.py:525
  246.8 5.9 %collective-permute-start.42 = (bf16[16,16,384]{2,1,0:T(8,128)(2,1)S(1)}, bf16[16,16,384]{2,1,0:T(8,128)(2,1)S(1)}, u32[]{:S(2)}, u32[]{:S(2)}) collective-permute-start(bf16[16,16,384]{2,1,0:T(8,128)(2,1)S(1)} %copy-done.37), channel_id=1, source_target_pairs={{0,1},{1,0},{2,3},{3,2},{4,5},{5,4},{6,7},{7,6},{8,9},{9,8},{10,11... | collective-permute-start | bytes 589832 | tf_op jit(solution)/shard_map/ppermute | solution.py:525
  249.0 6.1 %collective-permute-start.54 = (bf16[16,16,384]{2,1,0:T(8,128)(2,1)}, bf16[16,16,384]{2,1,0:T(8,128)(2,1)S(1)}, u32[]{:S(2)}, u32[]{:S(2)}) collective-permute-start(bf16[16,16,384]{2,1,0:T(8,128)(2,1)} %get-tuple-element.97), channel_id=1, source_target_pairs={{0,1},{1,0},{2,3},{3,2},{4,5},{5,4},{6,7},{7,6},{8,9},{9,8},{10,11... | collective-permute-start | bytes 589832 | tf_op jit(solution)/shard_map/ppermute | solution.py:525
  254.1 7.9 %collective-permute-start.82 = (f32[14464]{0:T(1024)S(1)}, f32[14464]{0:T(1024)S(1)}, u32[]{:S(2)}, u32[]{:S(2)}) collective-permute-start(f32[14464]{0:T(1024)S(1)} %add.296), channel_id=1, source_target_pairs={{0,16},{4,20},{8,24},{12,28},{16,0},{20,4},{24,8},{28,12},{1,17},{... | collective-permute-start | bytes 173576 | tf_op jit(solution)/shard_map/ppermute | solution.py:525
  255.2 6.9 %collective-permute-start.83 = (f32[14464]{0:T(1024)S(1)}, f32[14464]{0:T(1024)S(1)}, u32[]{:S(2)}, u32[]{:S(2)}) collective-permute-start(f32[14464]{0:T(1024)S(1)} %add.296), channel_id=1, source_target_pairs={{0,24},{4,28},{8,16},{12,20},{16,8},{20,12},{24,0},{28,4},{1,25},{... | collective-permute-start | bytes 173576 | tf_op jit(solution)/shard_map/ppermute | solution.py:525
  257.5 6.6 %collective-permute-start.60 = (bf16[16,16,512]{2,1,0:T(8,128)(2,1)S(1)}, bf16[16,16,512]{2,1,0:T(8,128)(2,1)S(1)}, u32[]{:S(2)}, u32[]{:S(2)}) collective-permute-start(bf16[16,16,512]{2,1,0:T(8,128)(2,1)S(1)} %copy-done.36), channel_id=1, source_target_pairs={{0,1},{1,0},{2,3},{3,2},{4,5},{5,4},{6,7},{7,6},{8,9},{9,8},{10,11... | collective-permute-start | bytes 786440 | tf_op jit(solution)/shard_map/ppermute | solution.py:525
  262.0 32.2 %collective-permute-start.35 = (bf16[304,512]{1,0:T(8,128)(2,1)S(1)}, bf16[304,512]{1,0:T(8,128)(2,1)S(1)}, u32[]{:S(2)}, u32[]{:S(2)}) collective-permute-start(bf16[304,512]{1,0:T(8,128)(2,1)S(1)} %copy-done.31), channel_id=1, source_target_pairs={{0,3},{1,2},{2,1},{3,0},{4,7},{5,6},{6,5},{7,4},{8,11},{9,10},{10,... | collective-permute-start | bytes 933896 | tf_op jit(solution)/shard_map/ppermute | solution.py:525
  262.1 32.8 %collective-permute-start.34 = (bf16[304,512]{1,0:T(8,128)(2,1)S(1)}, bf16[304,512]{1,0:T(8,128)(2,1)S(1)}, u32[]{:S(2)}, u32[]{:S(2)}) collective-permute-start(bf16[304,512]{1,0:T(8,128)(2,1)S(1)} %copy-done.29), channel_id=1, source_target_pairs={{0,2},{1,3},{2,0},{3,1},{4,6},{5,7},{6,4},{7,5},{8,10},{9,11},{10,... | collective-permute-start | bytes 933896 | tf_op jit(solution)/shard_map/ppermute | solution.py:525
  264.1 15.9 %collective-permute-start.37 = (bf16[8,16,384]{2,1,0:T(8,128)(2,1)S(1)}, bf16[8,16,384]{2,1,0:T(8,128)(2,1)S(1)}, u32[]{:S(2)}, u32[]{:S(2)}) collective-permute-start(bf16[8,16,384]{2,1,0:T(8,128)(2,1)S(1)} %slice.515), channel_id=1, source_target_pairs={{0,2},{1,3},{2,0},{3,1},{4,6},{5,7},{6,4},{7,5},{8,10},{9,11},{10,... | collective-permute-start | bytes 294920 | tf_op jit(solution)/shard_map/ppermute | solution.py:525
  294.9 10.3 %collective-permute-start.31 = (bf16[304,512]{1,0:T(8,128)(2,1)S(1)}, bf16[304,512]{1,0:T(8,128)(2,1)S(1)}, u32[]{:S(2)}, u32[]{:S(2)}) collective-permute-start(bf16[304,512]{1,0:T(8,128)(2,1)S(1)} %copy-done.26), channel_id=1, source_target_pairs={{0,2},{1,3},{2,0},{3,1},{4,6},{5,7},{6,4},{7,5},{8,10},{9,11},{10,... | collective-permute-start | bytes 933896 | tf_op jit(solution)/shard_map/ppermute | solution.py:525
  295.7 14.2 %collective-permute-start.32 = (bf16[304,512]{1,0:T(8,128)(2,1)S(1)}, bf16[304,512]{1,0:T(8,128)(2,1)S(1)}, u32[]{:S(2)}, u32[]{:S(2)}) collective-permute-start(bf16[304,512]{1,0:T(8,128)(2,1)S(1)} %copy-done.25), channel_id=1, source_target_pairs={{0,3},{1,2},{2,1},{3,0},{4,7},{5,6},{6,5},{7,4},{8,11},{9,10},{10,... | collective-permute-start | bytes 933896 | tf_op jit(solution)/shard_map/ppermute | solution.py:525
  297.0 16.7 %collective-permute-start.38 = (bf16[4,16,384]{2,1,0:T(8,128)(2,1)S(1)}, bf16[4,16,384]{2,1,0:T(8,128)(2,1)S(1)}, u32[]{:S(2)}, u32[]{:S(2)}) collective-permute-start(bf16[4,16,384]{2,1,0:T(8,128)(2,1)S(1)} %slice.520), channel_id=1, source_target_pairs={{0,4},{4,0},{8,12},{12,8},{16,20},{20,16},{24,28},{28,24},{1,5},{5... | collective-permute-start | bytes 147464 | tf_op jit(solution)/shard_map/ppermute | solution.py:525
  305.2 9.6 %collective-permute-start.44 = (bf16[4,16,384]{2,1,0:T(8,128)(2,1)S(1)}, bf16[4,16,384]{2,1,0:T(8,128)(2,1)S(1)}, u32[]{:S(2)}, u32[]{:S(2)}) collective-permute-start(bf16[4,16,384]{2,1,0:T(8,128)(2,1)S(1)} %slice.519), channel_id=1, source_target_pairs={{0,2},{1,3},{2,0},{3,1},{4,6},{5,7},{6,4},{7,5},{8,10},{9,11},{10,... | collective-permute-start | bytes 147464 | tf_op jit(solution)/shard_map/ppermute | solution.py:525
  318.3 5.5 %collective-permute-start.41 = (bf16[16,384]{1,0:T(8,128)(2,1)S(1)}, bf16[16,384]{1,0:T(8,128)(2,1)S(1)}, u32[]{:S(2)}, u32[]{:S(2)}) collective-permute-start(bf16[16,384]{1,0:T(8,128)(2,1)S(1)} %get-tuple-element.256), channel_id=1, source_target_pairs={{0,24},{4,28},{8,16},{12,20},{16,8},{20,12},{24,0},{28,4},{1,25},{... | collective-permute-start | bytes 36872 | tf_op jit(solution)/shard_map/ppermute | solution.py:525
  320.2 6.1 %collective-permute-start.45 = (bf16[16,384]{1,0:T(8,128)(2,1)S(1)}, bf16[16,384]{1,0:T(8,128)(2,1)S(1)}, u32[]{:S(2)}, u32[]{:S(2)}) collective-permute-start(bf16[16,384]{1,0:T(8,128)(2,1)S(1)} %get-tuple-element.258), channel_id=1, source_target_pairs={{0,8},{4,12},{8,0},{12,4},{16,24},{20,28},{24,16},{28,20},{1,9},{5... | collective-permute-start | bytes 36872 | tf_op jit(solution)/shard_map/ppermute | solution.py:525
  320.3 6.0 %collective-permute-start.46 = (bf16[16,384]{1,0:T(8,128)(2,1)S(1)}, bf16[16,384]{1,0:T(8,128)(2,1)S(1)}, u32[]{:S(2)}, u32[]{:S(2)}) collective-permute-start(bf16[16,384]{1,0:T(8,128)(2,1)S(1)} %get-tuple-element.260), channel_id=1, source_target_pairs={{0,16},{4,20},{8,24},{12,28},{16,0},{20,4},{24,8},{28,12},{1,17},{... | collective-permute-start | bytes 36872 | tf_op jit(solution)/shard_map/ppermute | solution.py:525
  323.8 5.5 %collective-permute-start.47 = (bf16[16,384]{1,0:T(8,128)(2,1)S(1)}, bf16[16,384]{1,0:T(8,128)(2,1)S(1)}, u32[]{:S(2)}, u32[]{:S(2)}) collective-permute-start(bf16[16,384]{1,0:T(8,128)(2,1)S(1)} %get-tuple-element.259), channel_id=1, source_target_pairs={{0,24},{4,28},{8,16},{12,20},{16,8},{20,12},{24,0},{28,4},{1,25},{... | collective-permute-start | bytes 36872 | tf_op jit(solution)/shard_map/ppermute | solution.py:525
  326.3 5.5 %collective-permute-start.51 = (bf16[16,384]{1,0:T(8,128)(2,1)S(1)}, bf16[16,384]{1,0:T(8,128)(2,1)S(1)}, u32[]{:S(2)}, u32[]{:S(2)}) collective-permute-start(bf16[16,384]{1,0:T(8,128)(2,1)S(1)} %get-tuple-element.261), channel_id=1, source_target_pairs={{0,8},{4,12},{8,0},{12,4},{16,24},{20,28},{24,16},{28,20},{1,9},{5... | collective-permute-start | bytes 36872 | tf_op jit(solution)/shard_map/ppermute | solution.py:525
  326.3 7.1 %collective-permute-start.52 = (bf16[16,384]{1,0:T(8,128)(2,1)S(1)}, bf16[16,384]{1,0:T(8,128)(2,1)S(1)}, u32[]{:S(2)}, u32[]{:S(2)}) collective-permute-start(bf16[16,384]{1,0:T(8,128)(2,1)S(1)} %get-tuple-element.263), channel_id=1, source_target_pairs={{0,16},{4,20},{8,24},{12,28},{16,0},{20,4},{24,8},{28,12},{1,17},{... | collective-permute-start | bytes 36872 | tf_op jit(solution)/shard_map/ppermute | solution.py:525
  329.2 5.5 %collective-permute-start.53 = (bf16[16,384]{1,0:T(8,128)(2,1)S(1)}, bf16[16,384]{1,0:T(8,128)(2,1)S(1)}, u32[]{:S(2)}, u32[]{:S(2)}) collective-permute-start(bf16[16,384]{1,0:T(8,128)(2,1)S(1)} %get-tuple-element.262), channel_id=1, source_target_pairs={{0,24},{4,28},{8,16},{12,20},{16,8},{20,12},{24,0},{28,4},{1,25},{... | collective-permute-start | bytes 36872 | tf_op jit(solution)/shard_map/ppermute | solution.py:525
  333.4 5.9 %collective-permute-start.57 = (bf16[16,384]{1,0:T(8,128)(2,1)S(1)}, bf16[16,384]{1,0:T(8,128)(2,1)S(1)}, u32[]{:S(2)}, u32[]{:S(2)}) collective-permute-start(bf16[16,384]{1,0:T(8,128)(2,1)S(1)} %get-tuple-element.264), channel_id=1, source_target_pairs={{0,8},{4,12},{8,0},{12,4},{16,24},{20,28},{24,16},{28,20},{1,9},{5... | collective-permute-start | bytes 36872 | tf_op jit(solution)/shard_map/ppermute | solution.py:525
  339.3 9.0 %collective-permute-start.62 = (bf16[4,16,512]{2,1,0:T(8,128)(2,1)}, bf16[4,16,512]{2,1,0:T(8,128)(2,1)}, u32[]{:S(2)}, u32[]{:S(2)}) collective-permute-start(bf16[4,16,512]{2,1,0:T(8,128)(2,1)} %slice.516), channel_id=1, source_target_pairs={{0,2},{1,3},{2,0},{3,1},{4,6},{5,7},{6,4},{7,5},{8,10},{9,11},{10,... | collective-permute-start | bytes 196616 | tf_op jit(solution)/shard_map/ppermute | solution.py:525
  352.9 5.5 %collective-permute-start.65 = (bf16[16,512]{1,0:T(8,128)(2,1)S(1)}, bf16[16,512]{1,0:T(8,128)(2,1)S(1)}, u32[]{:S(2)}, u32[]{:S(2)}) collective-permute-start(bf16[16,512]{1,0:T(8,128)(2,1)S(1)} %get-tuple-element.243), channel_id=1, source_target_pairs={{0,24},{4,28},{8,16},{12,20},{16,8},{20,12},{24,0},{28,4},{1,25},{... | collective-permute-start | bytes 49160 | tf_op jit(solution)/shard_map/ppermute | solution.py:525
  363.1 16.5 %collective-permute-start.67 = (bf16[8,16,3200]{2,1,0:T(8,128)(2,1)S(1)}, bf16[8,16,3200]{2,1,0:T(8,128)(2,1)S(1)}, u32[]{:S(2)}, u32[]{:S(2)}) collective-permute-start(bf16[8,16,3200]{2,1,0:T(8,128)(2,1)S(1)} %slice.508), channel_id=1, source_target_pairs={{0,2},{1,3},{2,0},{3,1},{4,6},{5,7},{6,4},{7,5},{8,10},{9,11},{10,... | collective-permute-start | bytes 2457608 | tf_op jit(solution)/shard_map/ppermute | solution.py:525
  364.8 18.2 %collective-permute-start.73 = (bf16[8,16,3200]{2,1,0:T(8,128)(2,1)S(1)}, bf16[8,16,3200]{2,1,0:T(8,128)(2,1)S(1)}, u32[]{:S(2)}, u32[]{:S(2)}) collective-permute-start(bf16[8,16,3200]{2,1,0:T(8,128)(2,1)S(1)} %slice.507), channel_id=1, source_target_pairs={{0,4},{4,0},{8,12},{12,8},{16,20},{20,16},{24,28},{28,24},{1,5},{5... | collective-permute-start | bytes 2457608 | tf_op jit(solution)/shard_map/ppermute | solution.py:525
  379.7 8.0 %collective-permute-start.68 = (bf16[4,16,3200]{2,1,0:T(8,128)(2,1)S(1)}, bf16[4,16,3200]{2,1,0:T(8,128)(2,1)S(1)}, u32[]{:S(2)}, u32[]{:S(2)}) collective-permute-start(bf16[4,16,3200]{2,1,0:T(8,128)(2,1)S(1)} %slice.510), channel_id=1, source_target_pairs={{0,4},{4,0},{8,12},{12,8},{16,20},{20,16},{24,28},{28,24},{1,5},{5... | collective-permute-start | bytes 1228808 | tf_op jit(solution)/shard_map/ppermute | solution.py:525
  383.2 9.1 %collective-permute-start.74 = (bf16[4,16,3200]{2,1,0:T(8,128)(2,1)S(1)}, bf16[4,16,3200]{2,1,0:T(8,128)(2,1)S(1)}, u32[]{:S(2)}, u32[]{:S(2)}) collective-permute-start(bf16[4,16,3200]{2,1,0:T(8,128)(2,1)S(1)} %slice.509), channel_id=1, source_target_pairs={{0,2},{1,3},{2,0},{3,1},{4,6},{5,7},{6,4},{7,5},{8,10},{9,11},{10,... | collective-permute-start | bytes 1228808 | tf_op jit(solution)/shard_map/ppermute | solution.py:525
  387.9 7.2 %collective-permute-start.69 = (bf16[16,3200]{1,0:T(8,128)(2,1)S(1)}, bf16[16,3200]{1,0:T(8,128)(2,1)S(1)}, u32[]{:S(2)}, u32[]{:S(2)}) collective-permute-start(bf16[16,3200]{1,0:T(8,128)(2,1)S(1)} %get-tuple-element.208), channel_id=1, source_target_pairs={{0,8},{4,12},{8,0},{12,4},{16,24},{20,28},{24,16},{28,20},{1,9},{5... | collective-permute-start | bytes 307208 | tf_op jit(solution)/shard_map/ppermute | solution.py:525
  387.9 9.4 %collective-permute-start.70 = (bf16[16,3200]{1,0:T(8,128)(2,1)S(1)}, bf16[16,3200]{1,0:T(8,128)(2,1)S(1)}, u32[]{:S(2)}, u32[]{:S(2)}) collective-permute-start(bf16[16,3200]{1,0:T(8,128)(2,1)S(1)} %get-tuple-element.210), channel_id=1, source_target_pairs={{0,16},{4,20},{8,24},{12,28},{16,0},{20,4},{24,8},{28,12},{1,17},{... | collective-permute-start | bytes 307208 | tf_op jit(solution)/shard_map/ppermute | solution.py:525
  390.4 6.9 %collective-permute-start.71 = (bf16[16,3200]{1,0:T(8,128)(2,1)S(1)}, bf16[16,3200]{1,0:T(8,128)(2,1)S(1)}, u32[]{:S(2)}, u32[]{:S(2)}) collective-permute-start(bf16[16,3200]{1,0:T(8,128)(2,1)S(1)} %get-tuple-element.209), channel_id=1, source_target_pairs={{0,24},{4,28},{8,16},{12,20},{16,8},{20,12},{24,0},{28,4},{1,25},{... | collective-permute-start | bytes 307208 | tf_op jit(solution)/shard_map/ppermute | solution.py:525
  392.5 5.9 %collective-permute-start.75 = (bf16[16,3200]{1,0:T(8,128)(2,1)S(1)}, bf16[16,3200]{1,0:T(8,128)(2,1)S(1)}, u32[]{:S(2)}, u32[]{:S(2)}) collective-permute-start(bf16[16,3200]{1,0:T(8,128)(2,1)S(1)} %get-tuple-element.211), channel_id=1, source_target_pairs={{0,8},{4,12},{8,0},{12,4},{16,24},{20,28},{24,16},{28,20},{1,9},{5... | collective-permute-start | bytes 307208 | tf_op jit(solution)/shard_map/ppermute | solution.py:525
  392.6 9.1 %collective-permute-start.76 = (bf16[16,3200]{1,0:T(8,128)(2,1)S(1)}, bf16[16,3200]{1,0:T(8,128)(2,1)S(1)}, u32[]{:S(2)}, u32[]{:S(2)}) collective-permute-start(bf16[16,3200]{1,0:T(8,128)(2,1)S(1)} %get-tuple-element.213), channel_id=1, source_target_pairs={{0,16},{4,20},{8,24},{12,28},{16,0},{20,4},{24,8},{28,12},{1,17},{... | collective-permute-start | bytes 307208 | tf_op jit(solution)/shard_map/ppermute | solution.py:525
  395.1 6.6 %collective-permute-start.77 = (bf16[16,3200]{1,0:T(8,128)(2,1)S(1)}, bf16[16,3200]{1,0:T(8,128)(2,1)S(1)}, u32[]{:S(2)}, u32[]{:S(2)}) collective-permute-start(bf16[16,3200]{1,0:T(8,128)(2,1)S(1)} %get-tuple-element.212), channel_id=1, source_target_pairs={{0,24},{4,28},{8,16},{12,20},{16,8},{20,12},{24,0},{28,4},{1,25},{... | collective-permute-start | bytes 307208 | tf_op jit(solution)/shard_map/ppermute | solution.py:525
  (62 other events, 649.8 us)
